TPU v7x, 32 devices: a whole 2x2x4 slice. The times are simulated.
32 devices in a mesh: dp: 16 (over z, y, core), tensor: 2 (over x).
Axes of the slice: x: 2, y: 2, z: 4, core: 2. Of those that a mesh axis runs over, the one named last changes fastest.
Arguments:
- tokens: bfloat16 [32768, 1024], P(('dp', 'tensor')), may hold values from -6 to 6
- gain_mix: float32 [1024], replicated, may hold values from 0.5 to 1.5
- proj_in: bfloat16 [1024, 3, 1024], P(None, None, 'tensor'), may hold values from -0.1875 to 0.1875
- conv_filter: float32 [3, 1024], P(None, 'tensor'), may hold values from -3.5 to 3.5
- proj_out: bfloat16 [1024, 1024], P('tensor'), may hold values from -0.1875 to 0.1875
- gain_ffn: float32 [1024], replicated, may hold values from 0.5 to 1.5
- w_gate: bfloat16 [1024, 4608], P(None, 'tensor'), may hold values from -0.1875 to 0.1875
- w_up: bfloat16 [1024, 4608], P(None, 'tensor'), may hold values from -0.1875 to 0.1875
- w_down: bfloat16 [4608, 1024], P('tensor'), may hold values from -0.125 to 0.125
- cotangent: bfloat16 [32768, 1024], P(('dp', 'tensor')), may hold values from -6 to 6
Outputs:
- output: bfloat16 [32768, 1024], P(('dp', 'tensor'))
- grad_tokens: float32 [32768, 1024], P(('dp', 'tensor'))
- grad_gain_mix: float32 [1024], replicated
- grad_proj_in: float32 [1024, 3, 1024], P(None, None, 'tensor')
- grad_conv_filter: float32 [3, 1024], P(None, 'tensor')
- grad_proj_out: float32 [1024, 1024], P('tensor')
- grad_gain_ffn: float32 [1024], replicated
- grad_w_gate: float32 [1024, 4608], P(None, 'tensor')
- grad_w_up: float32 [1024, 4608], P(None, 'tensor')
- grad_w_down: float32 [4608, 1024], P('tensor')
All inputs are finite; a program needn't handle non-finite values.
Results may differ from a plain program's by a relative error of at most 0.0099.
Values may be sent and summed in bfloat16 or wider, within the bound.
No kernel may reach another device: no remote copies, remote signals or barrier semaphores. Data moves between devices by JAX's collectives and lax.ppermute only.
A program may use at most 256 MiB of HBM per device.

v0:
```python
import jax
import jax.numpy as jnp
from jax import lax
from jax.sharding import PartitionSpec as P

LEN = 512


epsilon = 1e-05


def times_rows(left, right):
    return jnp.dot(left, right, preferred_element_type=jnp.float32)


def left_outer(left, right):
    return lax.dot_general(
        left, right, (((0,), (0,)), ((), ())), preferred_element_type=jnp.float32
    )


def right_outer(left, right):
    return lax.dot_general(
        left, right, (((1,), (1,)), ((), ())), preferred_element_type=jnp.float32
    )


def row_position(values):
    return lax.broadcasted_iota(jnp.int32, (values.shape[0], 1), 0) % LEN


def shift_down(values, steps):
    shifted = jnp.concatenate(
        [jnp.zeros((steps, values.shape[1]), values.dtype), values[:-steps]], 0
    )
    return jnp.where(row_position(values) >= steps, shifted, jnp.zeros_like(shifted))


def shift_up(values, steps):
    masked = jnp.where(row_position(values) >= steps, values, jnp.zeros_like(values))
    return jnp.concatenate([masked[steps:], jnp.zeros((steps, values.shape[1]), values.dtype)], 0)


def norm_back(grad_unit, unit, scale):
    return scale * (grad_unit - unit * jnp.mean(grad_unit * unit, axis=-1, keepdims=True))


def shards(
    tokens, gain_mix, proj_in, conv_filter, proj_out, gain_ffn, w_gate, w_up, w_down, cotangent
):
    model_width = tokens.shape[1]
    channels = proj_in.shape[2]
    resid_in = tokens.astype(jnp.float32)
    scale_mix = lax.rsqrt(jnp.mean(resid_in * resid_in, axis=-1, keepdims=True) + epsilon)
    unit_mix = resid_in * scale_mix
    normed = (unit_mix * gain_mix).astype(jnp.bfloat16)
    normed_all = lax.all_gather(normed, "tensor", axis=0, tiled=True)
    flat_in = proj_in.reshape(model_width, 3 * channels)
    projected = times_rows(normed_all, flat_in).reshape(-1, 3, channels)
    gate_b = projected[:, 0]
    gate_c = projected[:, 1]
    values = projected[:, 2]
    mixed_in = gate_b * values
    back_one = shift_down(mixed_in, 1)
    back_two = shift_down(mixed_in, 2)
    convolved = conv_filter[2] * mixed_in + conv_filter[1] * back_one + conv_filter[0] * back_two
    gated = (gate_c * convolved).astype(jnp.bfloat16)
    mixer = lax.psum_scatter(times_rows(gated, proj_out), "tensor", scatter_dimension=0, tiled=True)
    middle = resid_in + mixer
    scale_ffn = lax.rsqrt(jnp.mean(middle * middle, axis=-1, keepdims=True) + epsilon)
    unit_ffn = middle * scale_ffn
    normed_mid = (unit_ffn * gain_ffn).astype(jnp.bfloat16)
    grad_out = cotangent.astype(jnp.float32)
    mid_all = lax.all_gather(normed_mid, "tensor", axis=0, tiled=True)
    gate_value = times_rows(mid_all, w_gate)
    up_value = times_rows(mid_all, w_up)
    sigmoid_gate = jax.nn.sigmoid(gate_value)
    hidden = (gate_value * sigmoid_gate * up_value).astype(jnp.bfloat16)
    branch = lax.psum_scatter(times_rows(hidden, w_down), "tensor", scatter_dimension=0, tiled=True)
    cot_all = lax.all_gather(cotangent, "tensor", axis=0, tiled=True)
    grad_hidden = right_outer(cot_all, w_down)
    grad_gate = (
        grad_hidden * up_value * sigmoid_gate * (1.0 + gate_value * (1.0 - sigmoid_gate))
    ).astype(jnp.bfloat16)
    grad_upper = (grad_hidden * gate_value * sigmoid_gate).astype(jnp.bfloat16)
    grad_w_down = left_outer(hidden, cot_all)
    grad_w_gate = left_outer(mid_all, grad_gate)
    grad_w_up = left_outer(mid_all, grad_upper)
    grad_mid = lax.psum_scatter(
        right_outer(grad_gate, w_gate) + right_outer(grad_upper, w_up),
        "tensor",
        scatter_dimension=0,
        tiled=True,
    )
    output = (middle + branch).astype(jnp.bfloat16)
    grad_gain_ffn = jnp.sum(grad_mid * unit_ffn, axis=0)
    grad_middle = grad_out + norm_back(grad_mid * gain_ffn, unit_ffn, scale_ffn)
    mixer_cot = grad_middle.astype(jnp.bfloat16)
    cot_mix_all = lax.all_gather(mixer_cot, "tensor", axis=0, tiled=True)
    grad_proj_out = left_outer(gated, cot_mix_all)
    grad_gated = right_outer(cot_mix_all, proj_out)
    grad_cgate = grad_gated * convolved
    grad_conv = grad_gated * gate_c
    grad_conv_filter = jnp.stack(
        [
            jnp.sum(grad_conv * back_two, axis=0),
            jnp.sum(grad_conv * back_one, axis=0),
            jnp.sum(grad_conv * mixed_in, axis=0),
        ],
        0,
    )
    grad_mixed = (
        conv_filter[2] * grad_conv
        + conv_filter[1] * shift_up(grad_conv, 1)
        + conv_filter[0] * shift_up(grad_conv, 2)
    )
    grad_proj = (
        jnp.stack([grad_mixed * values, grad_cgate, grad_mixed * gate_b], 1)
        .astype(jnp.bfloat16)
        .reshape(-1, 3 * channels)
    )
    grad_proj_in = left_outer(normed_all, grad_proj).reshape(model_width, 3, channels)
    grad_normed = lax.psum_scatter(
        right_outer(grad_proj, flat_in), "tensor", scatter_dimension=0, tiled=True
    )
    grad_gain_mix = jnp.sum(grad_normed * unit_mix, axis=0)
    grad_tokens = grad_middle + norm_back(grad_normed * gain_mix, unit_mix, scale_mix)
    grad_gain_mix, grad_gain_ffn = lax.psum((grad_gain_mix, grad_gain_ffn), ("dp", "tensor"))
    grad_proj_in, grad_conv_filter, grad_proj_out, grad_w_gate, grad_w_up, grad_w_down = lax.psum(
        (grad_proj_in, grad_conv_filter, grad_proj_out, grad_w_gate, grad_w_up, grad_w_down), "dp"
    )
    return (
        output,
        grad_tokens,
        grad_gain_mix,
        grad_proj_in,
        grad_conv_filter,
        grad_proj_out,
        grad_gain_ffn,
        grad_w_gate,
        grad_w_up,
        grad_w_down,
    )


def solution(mesh):
    placed = (
        P(("dp", "tensor"), None),
        P(),
        P(None, None, "tensor"),
        P(None, "tensor"),
        P("tensor", None),
        P(),
        P(None, "tensor"),
        P(None, "tensor"),
        P("tensor", None),
        P(("dp", "tensor"), None),
    )
    return jax.shard_map(
        shards,
        mesh=mesh,
        in_specs=placed,
        out_specs=(
            P(("dp", "tensor"), None),
            P(("dp", "tensor"), None),
            P(),
            P(None, None, "tensor"),
            P(None, "tensor"),
            P("tensor", None),
            P(),
            P(None, "tensor"),
            P(None, "tensor"),
            P("tensor", None),
        ),
        check_vma=False,
    )
```

profile of v0, /device:TPU:0, one launch (start us, length us, event | category | flops | bytes accessed | tf_op | source)
XLA Modules:
  0.0 1450.0 jit_solution(6464870816716236348)
XLA Ops:
  13.5 4.6 copy.22
  18.2 54.8 %all-gather.5.cloned.1.call-done = bf16[2048,1024]{1,0:T(8,128)(2,1)} async-done(((bf16[1024,1024]{1,0:T(8,128)(2,1)}), bf16[2048,1024]{1,0:T(8,128)(2,1)}) %all-gather.5.cloned.1.call-update) | async-done | bytes 4194320 | tf_op jit(solution)/shard_map/all_gather | solution.py:57
  73.1 9.6 fusion.14
  87.3 4.7 multiply_convert_fusion.4
  93.3 5.8 fusion.27
  99.2 99.3 %reduce-scatter.5.cloned.1.call-done = f32[1024,1024]{1,0:T(8,128)} async-done(((f32[2048,1024]{1,0:T(8,128)}), f32[1024,1024]{1,0:T(8,128)}) %reduce-scatter.5.cloned.1.call-update) | async-done | bytes 4194320 | tf_op jit(solution)/shard_map/reduce_scatter | solution.py:68
  206.2 56.0 %all-gather.7.cloned.1.call-done = bf16[2048,1024]{1,0:T(8,128)(2,1)} async-done(((bf16[1024,1024]{1,0:T(8,128)(2,1)}), bf16[2048,1024]{1,0:T(8,128)(2,1)}) %all-gather.7.cloned.1.call-update) | async-done | bytes 4194320 | tf_op jit(solution)/shard_map/all_gather | solution.py:74
  262.2 16.9 %fusion.28 = f32[2048,2304]{1,0:T(8,128)} fusion(bf16[2048,1024]{1,0:T(8,128)(2,1)} %all-gather.7.cloned.1.call-done, bf16[1024,2304]{1,0:T(8,128)(2,1)} %param.16), kind=kOutput, calls=%fused_computation.66 | convolution fusion | flops 9663676416 | bytes 27787264 | tf_op jit(solution)/shard_map/dot_general | solution.py:13
  279.0 15.4 %fusion.29 = f32[2048,2304]{1,0:T(8,128)} fusion(bf16[2048,1024]{1,0:T(8,128)(2,1)S(1)} %copy-done.39, bf16[1024,2304]{1,0:T(8,128)(2,1)} %param.17), kind=kOutput, calls=%fused_computation.67 | convolution fusion | flops 9663676416 | bytes 27787264 | tf_op jit(solution)/shard_map/dot_general | solution.py:13
  294.4 26.0 %all-gather.9.cloned.1.call-done = bf16[2048,1024]{1,0:T(8,128)(2,1)} async-done(((bf16[1024,1024]{1,0:T(8,128)(2,1)}), bf16[2048,1024]{1,0:T(8,128)(2,1)}) %all-gather.9.cloned.1.call-update) | async-done | bytes 4194320 | tf_op jit(solution)/shard_map/all_gather | solution.py:80
  320.4 35.7 %multiply_convert_fusion = (bf16[2048,2304]{1,0:T(8,128)(2,1)}, bf16[2048,2304]{1,0:T(8,128)(2,1)}, bf16[2048,2304]{1,0:T(8,128)(2,1)}) fusion(f32[2048,2304]{1,0:T(8,128)} %fusion.28, f32[2048,2304]{1,0:T(8,128)} %fusion.29, bf16[2048,1024]{1,0:T(8,128)(2,1)} %all-gather.9.cloned.1.call-done, bf16[2304,1024]{1,0:T(8,128)(2,1)} %param.18), kind=kOutput, calls=%fused_computation | convolution fusion | flops 9739173888 | bytes 74973184 | tf_op jit(solution)/shard_map/dot_general | solution.py:23
  356.1 16.1 %fusion.31 = f32[2048,1024]{1,0:T(8,128)} fusion(bf16[2048,2304]{1,0:T(8,128)(2,1)} %get-tuple-element.32, bf16[1024,2304]{1,0:T(8,128)(2,1)} %param.16), kind=kOutput, calls=%fused_computation.69 | convolution fusion | flops 9663676416 | bytes 22544384 | tf_op jit(solution)/shard_map/dot_general | solution.py:23
  372.2 15.8 %convolution_add_fusion = f32[2048,1024]{1,0:T(8,128)} fusion(f32[2048,1024]{1,0:T(8,128)} %fusion.31, bf16[2048,2304]{1,0:T(8,128)(2,1)S(1)} %copy-done.41, bf16[1024,2304]{1,0:T(8,128)(2,1)} %param.17), kind=kOutput, calls=%fused_computation.49 | convolution fusion | flops 9665773568 | bytes 30932992 | tf_op jit(solution)/shard_map/dot_general | solution.py:23
  388.1 99.3 %reduce-scatter.9.cloned.1.call-done = f32[1024,1024]{1,0:T(8,128)} async-done(((f32[2048,1024]{1,0:T(8,128)}), f32[1024,1024]{1,0:T(8,128)}) %reduce-scatter.9.cloned.1.call-update) | async-done | bytes 4194320 | tf_op jit(solution)/shard_map/reduce_scatter | solution.py:89
  487.4 4.7 multiply_reduce_fusion
  496.0 56.7 %all-gather.11.cloned.1.call-done = bf16[2048,1024]{1,0:T(8,128)(2,1)} async-done(((bf16[1024,1024]{1,0:T(8,128)(2,1)}), bf16[2048,1024]{1,0:T(8,128)(2,1)}) %all-gather.11.cloned.1.call-update) | async-done | bytes 4194320 | tf_op jit(solution)/shard_map/all_gather | solution.py:99
  552.7 11.4 multiply_reduce_fusion.3
  576.4 9.0 convolution_bitcast_fusion
  585.5 16.2 %fusion.30 = f32[2048,1024]{1,0:T(8,128)} fusion(bf16[2048,2304]{1,0:T(8,128)(2,1)} %get-tuple-element.33, bf16[2304,1024]{1,0:T(8,128)(2,1)} %param.18), kind=kOutput, calls=%fused_computation.68 | convolution fusion | flops 9663676416 | bytes 22544384 | tf_op jit(solution)/shard_map/dot_general | solution.py:13
  601.7 16.1 %fusion.35 = f32[2304,1024]{1,0:T(8,128)} fusion(bf16[2048,2304]{1,0:T(8,128)(2,1)} %get-tuple-element.33, bf16[2048,1024]{1,0:T(8,128)(2,1)} %all-gather.9.cloned.1.call-done), kind=kOutput, calls=%fused_computation.73 | convolution fusion | flops 9663676416 | bytes 23068672 | tf_op jit(solution)/shard_map/dot_general | solution.py:17
  617.9 14.6 %fusion.33 = f32[1024,2304]{1,0:T(8,128)} fusion(bf16[2048,1024]{1,0:T(8,128)(2,1)S(1)} %copy-done.40, bf16[2048,2304]{1,0:T(8,128)(2,1)} %get-tuple-element.32), kind=kOutput, calls=%fused_computation.71 | convolution fusion | flops 9663676416 | bytes 23068672 | tf_op jit(solution)/shard_map/dot_general | solution.py:17
  632.5 13.8 fusion.34
  650.0 8.8 fusion
  658.8 34.4 %psum.58 = f32[3,512]{1,0:T(4,128)} all-reduce(f32[3,512]{1,0:T(4,128)S(1)} %pad_maximum_fusion), channel_id=1, replica_groups=mesh['dp'=16,'tensor'=2] {'dp'}, use_global_device_ids=true, to_apply=%region_14.15 | all-reduce | flops 1536 | bytes 12288 | tf_op jit(solution)/shard_map/psum | solution.py:129
  696.8 37.7 %all-reduce.4 = (f32[1024]{0:T(1024)}, f32[1024]{0:T(1024)}) all-reduce(f32[1024]{0:T(1024)S(1)} %get-tuple-element.12, f32[1024]{0:T(1024)S(1)} %get-tuple-element.10), channel_id=1, replica_groups=mesh['dp'=16,'tensor'=2] {'dp','tensor'}, use_global_device_ids=true, to_apply=%region_9.10 | all-reduce | flops 2048 | bytes 16384 | tf_op jit(solution)/shard_map/psum | solution.py:128
  734.4 53.5 %reduce-scatter.7.cloned.1.call-done = f32[1024,1024]{1,0:T(8,128)} async-done(((f32[2048,1024]{1,0:T(8,128)}), f32[1024,1024]{1,0:T(8,128)}) %reduce-scatter.7.cloned.1.call-update) | async-done | bytes 4194320 | tf_op jit(solution)/shard_map/reduce_scatter | solution.py:79
  787.9 10.5 fusion.10
  798.4 618.3 %all-reduce.8.cloned.1.call-done = (f32[1024,3,512]{2,0,1:T(8,128)}, f32[512,1024]{1,0:T(8,128)}, f32[1024,2304]{1,0:T(8,128)}, f32[1024,2304]{1,0:T(8,128)}, f32[2304,1024]{1,0:T(8,128)}) async-done(((f32[1024,3,512]{2,0,1:T(8,128)}, f32[512,1024]{1,0:T(8,128)}, f32[1024,2304]{1,0:T(8,128)}, f32[1024,2304]{1,0:T(8,128)}, f32[2304,1024]{1,0:T(8,128)}), (f32[1024,3,512]{2,0,1:T(8,128)}, ...) | async-done | bytes 36700176 | tf_op jit(solution)/shard_map/psum | solution.py:129
  1416.7 6.9 copy.33
  1425.8 4.8 copy.35
  1430.6 8.8 copy.36
  1439.5 3.7 copy.37
  (147 shorter events, 45.5 us)
Async XLA Ops:
  7.2 86.2 %copy-start = (bf16[512,1024]{1,0:T(8,128)(2,1)S(1)}, bf16[512,1024]{1,0:T(8,128)(2,1)}, u32[]{:S(2)}) copy-start(bf16[512,1024]{1,0:T(8,128)(2,1)} %param.14) | copy-start | bytes 3145732
  7.2 65.9 %all-gather.5.cloned.1.call-start = ((), (), s32[]{:S(2)}) async-start(), calls=%async_computation.4 | async-start | bytes 6291456 | tf_op jit(solution)/shard_map/all_gather | solution.py:57
  13.5 185.1 %reduce-scatter.5.cloned.1.call-start = ((), (), s32[]{:S(2)}) async-start(), calls=%async_computation.5 | async-start | bytes 12582912 | tf_op jit(solution)/shard_map/reduce_scatter | solution.py:68
  18.2 65.7 %copy-start.27 = (pred[2048]{0:T(1024)(128)(4,1)}, pred[2048]{0:T(1024)(128)(4,1)S(1)}, u32[]{:S(2)}) copy-start(pred[2048]{0:T(1024)(128)(4,1)S(1)} %get-tuple-element.40) | copy-start | bytes 6148
  18.2 65.7 %copy-start.29 = (pred[2048]{0:T(1024)(128)(4,1)}, pred[2048]{0:T(1024)(128)(4,1)S(1)}, u32[]{:S(2)}) copy-start(pred[2048]{0:T(1024)(128)(4,1)S(1)} %get-tuple-element.41) | copy-start | bytes 6148
  18.2 65.6 %copy-start.31 = (f32[1,512]{1,0:T(1,128)}, f32[1,512]{1,0:T(1,128)S(1)}, u32[]{:S(2)}) copy-start(f32[1,512]{1,0:T(1,128)S(1)} %get-tuple-element.36) | copy-start | bytes 6148
  18.2 65.6 %copy-start.33 = (f32[1,512]{1,0:T(1,128)}, f32[1,512]{1,0:T(1,128)S(1)}, u32[]{:S(2)}) copy-start(f32[1,512]{1,0:T(1,128)S(1)} %get-tuple-element.37) | copy-start | bytes 6148
  18.2 65.6 %copy-start.35 = (f32[1,512]{1,0:T(1,128)}, f32[1,512]{1,0:T(1,128)S(1)}, u32[]{:S(2)}) copy-start(f32[1,512]{1,0:T(1,128)S(1)} %get-tuple-element.38) | copy-start | bytes 6148
  99.2 99.4 %copy-start.6 = (bf16[1024,1024]{1,0:T(8,128)(2,1)S(1)}, bf16[1024,1024]{1,0:T(8,128)(2,1)}, u32[]{:S(2)}) copy-start(bf16[1024,1024]{1,0:T(8,128)(2,1)} %param.10) | copy-start | bytes 6291460
  99.2 104.3 %copy-start.23 = (f32[1024]{0:T(1024)S(1)}, f32[1024]{0:T(1024)}, u32[]{:S(2)}) copy-start(f32[1024]{0:T(1024)} %param.15) | copy-start | bytes 12292
  99.2 163.0 %all-gather.7.cloned.1.call-start = ((), (), s32[]{:S(2)}) async-start(), calls=%async_computation.6 | async-start | bytes 6291456 | tf_op jit(solution)/shard_map/all_gather | solution.py:74
  205.3 115.2 %all-gather.9.cloned.1.call-start = ((), (), s32[]{:S(2)}) async-start(), calls=%async_computation.8 | async-start | bytes 6291456 | tf_op jit(solution)/shard_map/all_gather | solution.py:80
  205.8 281.6 %reduce-scatter.9.cloned.1.call-start = ((), (), s32[]{:S(2)}) async-start(), calls=%async_computation.9 | async-start | bytes 12582912 | tf_op jit(solution)/shard_map/reduce_scatter | solution.py:89
  262.2 16.9 %copy-start.39 = (bf16[2048,1024]{1,0:T(8,128)(2,1)S(1)}, bf16[2048,1024]{1,0:T(8,128)(2,1)}, u32[]{:S(2)}) copy-start(bf16[2048,1024]{1,0:T(8,128)(2,1)} %all-gather.7.cloned.1.call-done) | copy-start | bytes 12582916
  356.1 16.1 %copy-start.41 = (bf16[2048,2304]{1,0:T(8,128)(2,1)S(1)}, bf16[2048,2304]{1,0:T(8,128)(2,1)}, u32[]{:S(2)}) copy-start(bf16[2048,2304]{1,0:T(8,128)(2,1)} %get-tuple-element.31) | copy-start | bytes 28311556
  388.0 104.1 %copy-start.9 = (bf16[1024,1024]{1,0:T(8,128)(2,1)S(1)}, bf16[1024,1024]{1,0:T(8,128)(2,1)}, u32[]{:S(2)}) copy-start(bf16[1024,1024]{1,0:T(8,128)(2,1)} %param.19) | copy-start | bytes 6291460
  388.0 164.7 %all-gather.11.cloned.1.call-start = ((), (), s32[]{:S(2)}) async-start(), calls=%async_computation.10 | async-start | bytes 6291456 | tf_op jit(solution)/shard_map/all_gather | solution.py:99
  495.8 197.4 %reduce-scatter.11.cloned.1.call-start = ((), (), s32[]{:S(2)}) async-start(), calls=%async_computation.11 | async-start | bytes 12582912 | tf_op jit(solution)/shard_map/reduce_scatter | solution.py:123
  552.7 13.8 slice-start
  552.7 13.8 slice-start.1
  585.4 202.5 %reduce-scatter.7.cloned.1.call-start = ((), (), s32[]{:S(2)}) async-start(), calls=%async_computation.7 | async-start | bytes 12582912 | tf_op jit(solution)/shard_map/reduce_scatter | solution.py:79
  601.6 815.0 %all-reduce.8.cloned.1.call-start = ((), (), s32[]{:S(2)}) async-start(), calls=%async_computation.12 | async-start | bytes 73400320 | tf_op jit(solution)/shard_map/psum | solution.py:129
  601.7 16.2 %copy-start.40 = (bf16[2048,1024]{1,0:T(8,128)(2,1)S(1)}, bf16[2048,1024]{1,0:T(8,128)(2,1)}, u32[]{:S(2)}) copy-start(bf16[2048,1024]{1,0:T(8,128)(2,1)} %all-gather.7.cloned.1.call-done) | copy-start | bytes 12582916
  601.7 30.8 %slice-start.6 = ((s8[9437184]{0:T(1024)(128)(4,1)}), s8[4194304]{0:T(1024)(128)(4,1)S(1)}, s32[]{:S(2)}) async-start(s8[9437184]{0:T(1024)(128)(4,1)} %bitcast.101), calls=%async_computation.19 | async-start | bytes 8388608
  601.7 30.8 %slice-start.7 = ((s8[9437184]{0:T(1024)(128)(4,1)}), s8[4194304]{0:T(1024)(128)(4,1)S(1)}, s32[]{:S(2)}) async-start(s8[9437184]{0:T(1024)(128)(4,1)} %bitcast.101), calls=%async_computation.20 | async-start | bytes 8388608
  617.9 14.6 %slice-start.8 = ((s8[9437184]{0:T(1024)(128)(4,1)}), s8[1048576]{0:T(1024)(128)(4,1)S(1)}, s32[]{:S(2)}) async-start(s8[9437184]{0:T(1024)(128)(4,1)} %bitcast.101), calls=%async_computation.21 | async-start | bytes 2097152
  632.5 13.9 copy-start.13
  632.5 13.8 copy-start.16
  658.8 34.4 %copy-start.7 = (bf16[1024,1024]{1,0:T(8,128)(2,1)S(1)}, bf16[1024,1024]{1,0:T(8,128)(2,1)}, u32[]{:S(2)}) copy-start(bf16[1024,1024]{1,0:T(8,128)(2,1)} %param.10) | copy-start | bytes 6291460
  658.8 34.4 %copy-start.25 = (f32[1024]{0:T(1024)S(1)}, f32[1024]{0:T(1024)}, u32[]{:S(2)}) copy-start(f32[1024]{0:T(1024)} %copy-done.24) | copy-start | bytes 12292
  658.8 34.4 %copy-start.26 = (f32[1024]{0:T(1024)S(1)}, f32[1024]{0:T(1024)}, u32[]{:S(2)}) copy-start(f32[1024]{0:T(1024)} %param.11) | copy-start | bytes 12292
  1425.8 13.6 slice-start.4
  (28 other events, 114.6 us)
Sparse Core Ops, SparseCore 0:
  13.6 59.4 all-gather.4
  99.3 99.2 reduce-scatter.4
  205.4 56.7 all-gather.6
  263.6 56.7 all-gather.8
  388.2 99.2 reduce-scatter.8
  495.9 56.7 all-gather.10
  585.5 99.2 reduce-scatter.10
  687.2 100.6 reduce-scatter.6
  794.4 622.2 all-reduce.7
where the time goes:
time: 1460 us; the launch traced here: 1450 us
  waiting for transfers between devices  1060 us (73%)
  matrix products  209 us (14%)
  blocking collectives  72 us (5%)
  local copies, waits for them, and re-layouts  45.6 us (3%)
  other arithmetic  43.7 us (3%)
    psum x1, waiting for transfers between devices, shards(): lax.psum((grad_proj_in, grad_conv_filter, grad_proj_out, grad_w_gate, gra...  618 us
    reduce_scatter x1, waiting for transfers between devices, shards(): lax.psum_scatter(right_outer(grad_gate, w_gate) + right_outer(grad_upper,...  99.3 us
    reduce_scatter x1, waiting for transfers between devices, shards(): lax.psum_scatter(times_rows(gated, proj_out), 'tensor', scatter_dimension...  99.3 us
    dot_general x5, matrix products, right_outer(): lax.dot_general(left, right, (((1,), (1,)), ((), ())), preferred_element_...  88 us
    dot_general x5, matrix products, times_rows(): return jnp.dot(left, right, preferred_element_type=jnp.float32)  63.9 us
    dot_general x5, matrix products, left_outer(): lax.dot_general(left, right, (((0,), (0,)), ((), ())), preferred_element_...  57 us
    all_gather x1, waiting for transfers between devices, shards(): cot_mix_all = lax.all_gather(mixer_cot, 'tensor', axis=0, tiled=True)  56.7 us
    all_gather x1, waiting for transfers between devices, shards(): mid_all = lax.all_gather(normed_mid, 'tensor', axis=0, tiled=True)  56 us
  transfers between devices with their start and end apart: 9, of which 8 were waited for; matrix products, arithmetic and copies ran while one was open for 9% of the time, Pallas kernels for 0%

commit v1 on v0

--- a/solution.py
+++ b/solution.py
@@ -1,6 +1,10 @@
+import functools
+
 import jax
 import jax.numpy as jnp
 from jax import lax
+from jax.experimental import pallas as pl
+from jax.experimental.pallas import tpu as pltpu
 from jax.sharding import PartitionSpec as P
 
 LEN = 512
@@ -45,7 +49,7 @@
     return scale * (grad_unit - unit * jnp.mean(grad_unit * unit, axis=-1, keepdims=True))
 
 
-def shards(
+def split_shards(
     tokens, gain_mix, proj_in, conv_filter, proj_out, gain_ffn, w_gate, w_up, w_down, cotangent
 ):
     model_width = tokens.shape[1]
@@ -143,6 +147,344 @@
     )
 
 
+WIDE = 256
+ROW_TILE = 512
+GROUPS = (4, 5)
+MIB = 1024 * 1024
+
+
+def fits(sizes, args):
+    dp, tensor = sizes
+    tokens, proj_in, w_gate = args[0], args[2], args[6]
+    return (
+        tensor == 2
+        and dp & (dp - 1) == 0
+        and 2 <= dp <= 16
+        and tokens.shape[0] % LEN == 0
+        and tokens.shape[1] == 1024
+        and proj_in.shape[2] % 128 == 0
+        and w_gate.shape[1] == WIDE * sum(GROUPS)
+    )
+
+
+def ffn_body(first, *refs):
+    if first:
+        h, ht, e, et, wg, wu, wd, branch, grad_h, keep, send, zs, gg, gu = refs
+    else:
+        h, ht, e, et, wg, wu, wd, branch_in, grad_in, branch, grad_h, keep, send, zs, gg, gu = refs
+    rows, half, wide = h.shape[0], keep.shape[0], wg.shape[1]
+
+    @pl.when(pl.program_id(0) == 0)
+    def _():
+        if first:
+            branch[...] = jnp.zeros_like(branch)
+            grad_h[...] = jnp.zeros_like(grad_h)
+        else:
+            branch[...] = branch_in[...]
+            grad_h[...] = grad_in[...]
+
+    for start in range(0, rows, ROW_TILE):
+        r = pl.ds(start, ROW_TILE)
+        gate = times_rows(h[r, :], wg[...])
+        up = times_rows(h[r, :], wu[...])
+        grad_hidden = right_outer(e[r, :], wd[...])
+        s = jax.nn.sigmoid(gate)
+        gs = gate * s
+        hidden = (gs * up).astype(jnp.bfloat16)
+        grad_up = (grad_hidden * gs).astype(jnp.bfloat16)
+        grad_gate = (grad_hidden * up * (s + gs * (1.0 - s))).astype(jnp.bfloat16)
+        zs[r, :] = hidden
+        gg[r, :] = grad_gate
+        gu[r, :] = grad_up
+        branch[r, :] += times_rows(hidden, wd[...])
+        grad_h[r, :] += right_outer(grad_gate, wg[...]) + right_outer(grad_up, wu[...])
+    for out, base in ((keep, 0), (send, half)):
+        a = ht[pl.ds(base, half), :]
+        out[:, 0:wide] = times_rows(a, gg[...]).astype(jnp.bfloat16)
+        out[:, wide : 2 * wide] = times_rows(a, gu[...]).astype(jnp.bfloat16)
+        out[:, 2 * wide : 3 * wide] = times_rows(et[pl.ds(base, half), :], zs[...]).astype(jnp.bfloat16)
+
+
+def ffn_part(h, ht, e, et, wg, wu, wd, sums, gate_at, down_at, count):
+    rows, width = h.shape
+    first = sums is None
+
+    def whole(shape):
+        return pl.BlockSpec(shape, lambda j: (0, 0), pipeline_mode=pl.Buffered(1))
+
+    in_specs = [
+        whole((rows, width)),
+        whole((width, rows)),
+        whole((rows, width)),
+        whole((width, rows)),
+        pl.BlockSpec((width, WIDE), lambda j: (0, gate_at + j)),
+        pl.BlockSpec((width, WIDE), lambda j: (0, gate_at + j)),
+        pl.BlockSpec((WIDE, width), lambda j: (down_at + j, 0)),
+    ]
+    args = [h, ht, e, et, wg, wu, wd]
+    if not first:
+        in_specs += [whole((rows, width))] * 2
+        args += list(sums)
+    branch, grad_h, keep, send = pl.pallas_call(
+        functools.partial(ffn_body, first),
+        grid=(count,),
+        in_specs=in_specs,
+        out_specs=[pl.BlockSpec((rows, width), lambda j: (0, 0))] * 2
+        + [pl.BlockSpec((width // 2, 3 * WIDE), lambda j: (0, j))] * 2,
+        out_shape=[jax.ShapeDtypeStruct((rows, width), jnp.float32)] * 2
+        + [jax.ShapeDtypeStruct((width // 2, 3 * WIDE * count), jnp.bfloat16)] * 2,
+        scratch_shapes=[pltpu.VMEM((rows, WIDE), jnp.bfloat16)] * 3,
+        input_output_aliases={} if first else {7: 0, 8: 1},
+        compiler_params=pltpu.CompilerParams(vmem_limit_bytes=56 * MIB),
+        cost_estimate=pl.CostEstimate(
+            flops=20 * rows * width * WIDE * count,
+            bytes_accessed=12 * width * WIDE * count + 16 * rows * width,
+            transcendentals=rows * WIDE * count,
+        ),
+    )(*args)
+    return (branch, grad_h), (keep, send)
+
+
+def ffn_final_body(grads, *refs):
+    gate, up, down = refs[-3:]
+    gate[...] = grads[:, 0:WIDE].astype(jnp.float32)
+    up[...] = grads[:, WIDE : 2 * WIDE].astype(jnp.float32)
+    down[...] = grads[:, 2 * WIDE : 3 * WIDE].astype(jnp.float32).T
+
+
+def ffn_final(grads, totals, at, columns):
+    width = grads.shape[0]
+    count = grads.shape[1] // (3 * WIDE)
+    old = [] if totals is None else list(totals)
+    return pl.pallas_call(
+        ffn_final_body,
+        grid=(count,),
+        in_specs=[pl.BlockSpec((width, 3 * WIDE), lambda j: (0, j))]
+        + [pl.BlockSpec(memory_space=pl.ANY)] * len(old),
+        out_specs=[
+            pl.BlockSpec((width, WIDE), lambda j: (0, at + j)),
+            pl.BlockSpec((width, WIDE), lambda j: (0, at + j)),
+            pl.BlockSpec((WIDE, width), lambda j: (at + j, 0)),
+        ],
+        out_shape=[
+            jax.ShapeDtypeStruct((width, columns), jnp.float32),
+            jax.ShapeDtypeStruct((width, columns), jnp.float32),
+            jax.ShapeDtypeStruct((columns, width), jnp.float32),
+        ],
+        input_output_aliases={1 + i: i for i in range(len(old))},
+        compiler_params=pltpu.CompilerParams(vmem_limit_bytes=40 * MIB),
+        cost_estimate=pl.CostEstimate(
+            flops=0, bytes_accessed=18 * width * WIDE * count, transcendentals=0
+        ),
+    )(grads, *old)
+
+
+def swap(values, dp, bit):
+    return lax.ppermute(values, "dp", [(i, i ^ (1 << bit)) for i in range(dp)])
+
+
+def cross(values):
+    return lax.ppermute(values, "tensor", [(0, 1), (1, 0)])
+
+
+def add(*terms):
+    total = terms[0].astype(jnp.float32)
+    for term in terms[1:]:
+        total = total + term.astype(jnp.float32)
+    return total.astype(terms[0].dtype)
+
+
+def halve(terms, dp, bits):
+    for bit in bits:
+        half = terms[0].shape[0] // 2
+        got = swap(add(*[t[half:] for t in terms]), dp, bit)
+        terms = [add(*[t[:half] for t in terms]), got]
+    return add(*terms)
+
+
+def block_order(me, dp, width, bits):
+    rows = lax.broadcasted_iota(jnp.int32, (width, width), 0)
+    columns = lax.broadcasted_iota(jnp.int32, (width, width), 1)
+    size = width // dp
+    block = rows // size
+    owner = jnp.zeros_like(block)
+    for place, bit in enumerate(reversed(bits)):
+        owner = owner | (((block >> place) & 1) << bit)
+    return (columns == (owner ^ me) * size + rows % size).astype(jnp.bfloat16)
+
+
+def ordered(order, values):
+    return right_outer(order, values).astype(jnp.bfloat16)
+
+
+def mixer_forward(normed, flat_in, taps):
+    channels = taps.shape[1]
+    projected = times_rows(normed, flat_in)
+    gate_b = projected[:, :channels]
+    gate_c = projected[:, channels : 2 * channels]
+    values = projected[:, 2 * channels :]
+    mixed_in = gate_b * values
+    back_one = shift_down(mixed_in, 1)
+    back_two = shift_down(mixed_in, 2)
+    convolved = taps[2] * mixed_in + taps[1] * back_one + taps[0] * back_two
+    gated = (gate_c * convolved).astype(jnp.bfloat16)
+    return gate_b, gate_c, values, mixed_in, back_one, back_two, convolved, gated
+
+
+def mixer_backward(grad_gated, kept, taps):
+    gate_b, gate_c, values, mixed_in, back_one, back_two, convolved, _ = kept
+    grad_cgate = grad_gated * convolved
+    grad_conv = grad_gated * gate_c
+    grad_taps = jnp.stack(
+        [
+            jnp.sum(grad_conv * back_two, axis=0),
+            jnp.sum(grad_conv * back_one, axis=0),
+            jnp.sum(grad_conv * mixed_in, axis=0),
+        ],
+        0,
+    )
+    grad_mixed = taps[2] * grad_conv + taps[1] * shift_up(grad_conv, 1) + taps[0] * shift_up(grad_conv, 2)
+    grad_proj = jnp.concatenate(
+        [grad_mixed * values, grad_cgate, grad_mixed * gate_b], 1
+    ).astype(jnp.bfloat16)
+    return grad_taps, grad_proj
+
+
+def paired_shards(
+    dp, tokens, gain_mix, proj_in, taps, proj_out, gain_ffn, w_gate, w_up, w_down, cotangent
+):
+    me = lax.axis_index("dp")
+    core = me & 1
+    width = tokens.shape[1]
+    channels = proj_in.shape[2]
+    hidden = w_gate.shape[1]
+    bits = tuple(range(dp.bit_length() - 1))
+    flat_in = proj_in.reshape(width, 3 * channels)
+
+    def far_blocks(values):
+        size = values.shape[0] // dp
+        return cross(lax.dynamic_slice_in_dim(values, me * size, size, 0))
+
+    def gathered(blocks):
+        return lax.all_gather(blocks, "dp", axis=0, tiled=True)
+
+    in_blocks, out_blocks, down_blocks = far_blocks(flat_in), far_blocks(proj_out), far_blocks(w_down)
+    taps_far = cross(taps)
+    flat_in_far = gathered(in_blocks)
+    proj_out_far = gathered(out_blocks)
+    w_down_far = gathered(down_blocks)
+
+    def far_columns(values, at, count, after):
+        part = lax.dynamic_slice(values, (core * (width // 2), at), (width // 2, count))
+        part, _ = lax.optimization_barrier((part, after))
+        mine = cross(part)
+        other = swap(mine, dp, 0)
+        return jnp.concatenate([jnp.where(core == 0, mine, other), jnp.where(core == 0, other, mine)], 0)
+
+    far, at, after = [], 0, (in_blocks, out_blocks, down_blocks)
+    for count in GROUPS:
+        gate_far = far_columns(w_gate, at * WIDE, count * WIDE, after)
+        up_far = far_columns(w_up, at * WIDE, count * WIDE, after)
+        far.append((gate_far, up_far))
+        at += count
+
+    order = block_order(me, dp, width, bits)
+    cot_t = ordered(order, cotangent)
+
+    resid_in = tokens.astype(jnp.float32)
+    scale_mix = lax.rsqrt(jnp.mean(resid_in * resid_in, axis=-1, keepdims=True) + epsilon)
+    unit_mix = resid_in * scale_mix
+    normed = (unit_mix * gain_mix).astype(jnp.bfloat16)
+    normed_t = ordered(order, normed)
+    kept = mixer_forward(normed, flat_in, taps)
+    kept_far = mixer_forward(normed, flat_in_far, taps_far)
+    mixer = times_rows(kept[-1], proj_out) + times_rows(kept_far[-1], proj_out_far)
+    middle = resid_in + mixer
+    scale_ffn = lax.rsqrt(jnp.mean(middle * middle, axis=-1, keepdims=True) + epsilon)
+    unit_ffn = middle * scale_ffn
+    normed_mid = (unit_ffn * gain_ffn).astype(jnp.bfloat16)
+    normed_mid_t = ordered(order, normed_mid)
+
+    sums, near_grads, far_grads, at = None, [], [], 0
+    for count in GROUPS:
+        sums, grads = ffn_part(
+            normed_mid, normed_mid_t, cotangent, cot_t, w_gate, w_up, w_down, sums, at, at, count
+        )
+        near_grads.append(grads)
+        at += count
+    at = 0
+    for count, (gate_far, up_far) in zip(GROUPS, far):
+        sums, grads = ffn_part(
+            normed_mid, normed_mid_t, cotangent, cot_t, gate_far, up_far, w_down_far, sums, 0, at, count
+        )
+        far_grads.append(grads)
+        at += count
+
+    def reduced(near, far, far_first):
+        near = [near[0], swap(near[1], dp, bits[0])]
+        far = [far[0], swap(far[1], dp, bits[0])]
+        if far_first:
+            return gathered(halve(near + [cross(add(*far))], dp, bits[1:]))
+        return gathered(add(halve(near, dp, bits[1:]), cross(halve(far, dp, bits[1:]))))
+
+    totals, at = None, 0
+    for index, count in enumerate(GROUPS):
+        grads = reduced(near_grads[index], far_grads[index], FAR_FIRST[index])
+        totals = ffn_final(grads, totals, at, hidden)
+        at += count
+    grad_w_gate, grad_w_up, grad_w_down = totals
+
+    branch, grad_mid = sums
+    output = (middle + branch).astype(jnp.bfloat16)
+    grad_gain_ffn = jnp.sum(grad_mid * unit_ffn, axis=0)
+    grad_middle = cotangent.astype(jnp.float32) + norm_back(grad_mid * gain_ffn, unit_ffn, scale_ffn)
+    mixer_cot = grad_middle.astype(jnp.bfloat16)
+    mixer_cot_t = ordered(order, mixer_cot)
+    grad_taps, grad_proj = mixer_backward(right_outer(mixer_cot, proj_out), kept, taps)
+    grad_taps_far, grad_proj_far = mixer_backward(right_outer(mixer_cot, proj_out_far), kept_far, taps_far)
+
+    def mixer_grads(grad_proj, gated):
+        def rows(part):
+            return jnp.concatenate(
+                [times_rows(normed_t[part], grad_proj), times_rows(mixer_cot_t[part], gated)], 1
+            ).astype(jnp.bfloat16)
+
+        return rows(slice(0, width // 2)), rows(slice(width // 2, width))
+
+    grads = reduced(
+        mixer_grads(grad_proj, kept[-1]), mixer_grads(grad_proj_far, kept_far[-1]), FAR_FIRST[-1]
+    )
+    grad_proj_in = grads[:, : 3 * channels].astype(jnp.float32).reshape(width, 3, channels)
+    grad_proj_out = grads[:, 3 * channels :].astype(jnp.float32).T
+
+    grad_normed = right_outer(grad_proj, flat_in) + right_outer(grad_proj_far, flat_in_far)
+    grad_gain_mix = jnp.sum(grad_normed * unit_mix, axis=0)
+    grad_tokens = grad_middle + norm_back(grad_normed * gain_mix, unit_mix, scale_mix)
+
+    gains = jnp.concatenate([grad_gain_mix[None], grad_gain_ffn[None]], 0)
+    small = jnp.concatenate([gains[:, :channels], gains[:, channels:], grad_taps], 0)
+    small_far = jnp.concatenate([gains[:, :channels], gains[:, channels:], grad_taps_far], 0)
+    small = small + cross(small_far)
+    for bit in bits:
+        small = small + swap(small, dp, bit)
+    gains = jnp.concatenate([small[0:2], small[2:4]], 1)
+    return (
+        output,
+        grad_tokens,
+        gains[0],
+        grad_proj_in,
+        small[4:7],
+        grad_proj_out,
+        gains[1],
+        grad_w_gate,
+        grad_w_up,
+        grad_w_down,
+    )
+
+
+FAR_FIRST = (True, False, True)
+
+
 def solution(mesh):
     placed = (
         P(("dp", "tensor"), None),
@@ -156,8 +498,15 @@
         P("tensor", None),
         P(("dp", "tensor"), None),
     )
+    sizes = (mesh.shape["dp"], mesh.shape["tensor"])
+
+    def block(*args):
+        if fits(sizes, args):
+            return paired_shards(sizes[0], *args)
+        return split_shards(*args)
+
     return jax.shard_map(
-        shards,
+        block,
         mesh=mesh,
         in_specs=placed,
         out_specs=(

time: 1460 us -> 837 us (0.57)
  waiting for transfers between devices: 1060 us -> 452 us
  matrix products: 209 us -> 64.3 us
  Pallas kernels: 0 us -> 138 us
  blocking collectives: 72 us -> 0 us
  other arithmetic: 43.7 us -> 78.3 us
  starting transfers between devices: 0.66 us -> 31.4 us
    psum x1 -> x0, waiting for transfers between devices: 618 us -> none  [shards(): lax.psum((grad_proj_in, grad_conv_filter, grad_proj_out, grad_w_gate, gra...]
    ppermute x0 -> x38, waiting for transfers between devices: none -> 444 us  [the longest x26 256 us: swap(): return lax.ppermute(values, 'dp', [(i, i ^ 1 << bit) for i in range(dp)])]
    reduce_scatter x4 -> x0, waiting for transfers between devices: 252 us -> none  [the longest x1 99.3 us: shards(): lax.psum_scatter(right_outer(grad_gate, w_gate) + right_outer(grad_upper,...]
    all_gather x4 -> x6, waiting for transfers between devices: 193 us -> 8.2 us  [gathered(): return lax.all_gather(blocks, 'dp', axis=0, tiled=True)]
    pallas_call x0 -> x6, Pallas kernels: none -> 138 us  [the longest x4 127 us: ffn_part(): pl.pallas_call(functools.partial(ffn_body, first), grid=(count,), in_spec...]
    psum x2 -> x0, blocking collectives: 72 us -> none  [the longest x1 37.7 us: shards(): lax.psum((grad_gain_mix, grad_gain_ffn), ('dp', 'tensor'))]
    dot_general x5 -> x0, matrix products: 57 us -> none  [left_outer(): lax.dot_general(left, right, (((0,), (0,)), ((), ())), preferred_element_...]
    dot_general x5 -> x8, matrix products: 88 us -> 36.5 us  [right_outer(): lax.dot_general(left, right, (((1,), (1,)), ((), ())), preferred_element_...]
  transfers between devices with their start and end apart: 9 -> 44, of which waited for: 8 -> 22; matrix products, arithmetic and copies ran while one was open for 9% -> 16% of each run, Pallas kernels for 0% -> 8%
where the time goes in v1:
time: 837 us; the launch traced here: 829 us
  waiting for transfers between devices  452 us (54%)
  Pallas kernels  138 us (16%)
  other arithmetic  78.3 us (9%)
  matrix products  64.3 us (8%)
  local copies, waits for them, and re-layouts  49.5 us (6%)
  starting transfers between devices  31.4 us (4%)
  between operations  15.7 us (2%)
    ppermute x26, waiting for transfers between devices, swap(): return lax.ppermute(values, 'dp', [(i, i ^ 1 << bit) for i in range(dp)])  256 us
    ppermute x12, waiting for transfers between devices, cross(): return lax.ppermute(values, 'tensor', [(0, 1), (1, 0)])  187 us
    pallas_call x4, Pallas kernels, ffn_part(): pl.pallas_call(functools.partial(ffn_body, first), grid=(count,), in_spec...  127 us
    dot_general x8, matrix products, right_outer(): lax.dot_general(left, right, (((1,), (1,)), ((), ())), preferred_element_...  36.5 us
    unnamed x133, local copies, waits for them, and re-layouts  30.6 us
    dot_general x12, matrix products, times_rows(): return jnp.dot(left, right, preferred_element_type=jnp.float32)  27.7 us
    convert_element_type x18, other arithmetic, add(): return total.astype(terms[0].dtype)  22.3 us
    ppermute x26, starting transfers between devices, swap(): return lax.ppermute(values, 'dp', [(i, i ^ 1 << bit) for i in range(dp)])  17.6 us
  transfers between devices with their start and end apart: 44, of which 22 were waited for; matrix products, arithmetic and copies ran while one was open for 16% of the time, Pallas kernels for 8%

profile of v1, /device:TPU:0, one launch (start us, length us, event | category | flops | bytes accessed | tf_op | source)
XLA Modules:
  0.0 828.6 jit_solution(8086258068825563793)
XLA Ops:
  16.3 9.1 %collective-permute-done = bf16[64,1536]{0,1:T(8,128)(2,1)S(1)} collective-permute-done((bf16[64,1536]{0,1:T(8,128)(2,1)S(1)}, bf16[64,1536]{0,1:T(8,128)(2,1)S(1)}, u32[]{:S(2)}, u32[]{:S(2)}) %collective-permute-start) | collective-permute-done | bytes 196640 | tf_op jit(solution)/shard_map/ppermute | solution.py:287
  40.8 6.0 convolution_convert_fusion.6.refs_3_
  53.6 13.3 %collective-permute-done.8 = bf16[512,1024]{1,0:T(8,128)(2,1)} collective-permute-done((bf16[512,1024]{1,0:T(8,128)(2,1)}, bf16[512,1024]{1,0:T(8,128)(2,1)}, u32[]{:S(2)}, u32[]{:S(2)}) %collective-permute-start.8) | collective-permute-done | bytes 1048608 | tf_op jit(solution)/shard_map/ppermute | solution.py:287
  70.4 18.9 %collective-permute-done.10 = bf16[512,1024]{1,0:T(8,128)(2,1)} collective-permute-done((bf16[512,1024]{1,0:T(8,128)(2,1)}, bf16[512,1024]{1,0:T(8,128)(2,1)}, u32[]{:S(2)}, u32[]{:S(2)}) %collective-permute-start.10) | collective-permute-done | bytes 1048608 | tf_op jit(solution)/shard_map/ppermute | solution.py:287
  89.9 27.5 %collective-permute-done.4 = bf16[512,1280]{1,0:T(8,128)(2,1)} collective-permute-done((bf16[512,1280]{1,0:T(8,128)(2,1)S(1)}, bf16[512,1280]{1,0:T(8,128)(2,1)}, u32[]{:S(2)}, u32[]{:S(2)}) %collective-permute-start.4) | collective-permute-done | bytes 1310752 | tf_op jit(solution)/shard_map/ppermute | solution.py:287
  119.0 23.6 %collective-permute-done.6 = bf16[512,1280]{1,0:T(8,128)(2,1)} collective-permute-done((bf16[512,1280]{1,0:T(8,128)(2,1)}, bf16[512,1280]{1,0:T(8,128)(2,1)}, u32[]{:S(2)}, u32[]{:S(2)}) %collective-permute-start.6) | collective-permute-done | bytes 1310752 | tf_op jit(solution)/shard_map/ppermute | solution.py:287
  155.9 6.0 fusion.55
  164.7 6.4 multiply_convert_fusion.7
  187.0 27.1 %shard_map.177 = (f32[1024,1024]{1,0:T(8,128)}, f32[1024,1024]{1,0:T(8,128)}, bf16[512,3072]{1,0:T(8,128)(2,1)}, bf16[512,3072]{1,0:T(8,128)(2,1)}) custom-call(bf16[1024,1024]{1,0:T(8,128)(2,1)} %copy-done.21, bf16[1024,1024]{1,0:T(8,128)(2,1)} %convolution_convert_fusion.7.refs_1_, bf16[1024,1024]{1,0:T(8,128)(2,1)} %refs_2_.7, ...), custom_call_target="tpu_custom_call" | custom-call | flops 21474836480 | bytes 29360128 | tf_op jit(solution)/shard_map/pallas_call | solution.py:228
  214.1 34.9 %shard_map.178 = (f32[1024,1024]{1,0:T(8,128)}, f32[1024,1024]{1,0:T(8,128)}, bf16[512,3840]{1,0:T(8,128)(2,1)}, bf16[512,3840]{1,0:T(8,128)(2,1)}) custom-call(bf16[1024,1024]{1,0:T(8,128)(2,1)} %copy-done.21, bf16[1024,1024]{1,0:T(8,128)(2,1)} %convolution_convert_fusion.7.refs_1_, ...), custom_call_target="tpu_custom_call", output_to_operand_aliasing={{0}: (7, {}), {1}: (8, {})} | custom-call | flops 26843545600 | bytes 32505856 | tf_op jit(solution)/shard_map/pallas_call | solution.py:228
  249.0 29.5 %shard_map.179 = (f32[1024,1024]{1,0:T(8,128)}, f32[1024,1024]{1,0:T(8,128)}, bf16[512,3072]{1,0:T(8,128)(2,1)}, bf16[512,3072]{1,0:T(8,128)(2,1)}) custom-call(bf16[1024,1024]{1,0:T(8,128)(2,1)} %copy-done.21, bf16[1024,1024]{1,0:T(8,128)(2,1)} %convolution_convert_fusion.7.refs_1_, ...), custom_call_target="tpu_custom_call", output_to_operand_aliasing={{0}: (7, {}), {1}: (8, {})} | custom-call | flops 21474836480 | bytes 29360128 | tf_op jit(solution)/shard_map/pallas_call | solution.py:228
  278.5 35.3 %shard_map.180 = (f32[1024,1024]{1,0:T(8,128)}, f32[1024,1024]{1,0:T(8,128)}, bf16[512,3840]{1,0:T(8,128)(2,1)}, bf16[512,3840]{1,0:T(8,128)(2,1)}) custom-call(bf16[1024,1024]{1,0:T(8,128)(2,1)} %copy-done.21, bf16[1024,1024]{1,0:T(8,128)(2,1)} %convolution_convert_fusion.7.refs_1_, ...), custom_call_target="tpu_custom_call", output_to_operand_aliasing={{0}: (7, {}), {1}: (8, {})} | custom-call | flops 26843545600 | bytes 32505856 | tf_op jit(solution)/shard_map/pallas_call | solution.py:228
  332.2 7.4 multiply_reduce_fusion.6
  364.0 43.9 %collective-permute-done.19 = bf16[512,2048]{1,0:T(8,128)(2,1)S(1)} collective-permute-done((bf16[512,2048]{1,0:T(8,128)(2,1)S(1)}, bf16[512,2048]{1,0:T(8,128)(2,1)S(1)}, u32[]{:S(2)}, u32[]{:S(2)}) %collective-permute-start.19) | collective-permute-done | bytes 2097184 | tf_op jit(solution)/shard_map/ppermute | solution.py:287
  410.8 22.8 %collective-permute-done.20 = bf16[256,2048]{1,0:T(8,128)(2,1)S(1)} collective-permute-done((bf16[256,2048]{1,0:T(8,128)(2,1)S(1)}, bf16[256,2048]{1,0:T(8,128)(2,1)S(1)}, u32[]{:S(2)}, u32[]{:S(2)}) %collective-permute-start.20) | collective-permute-done | bytes 1048608 | tf_op jit(solution)/shard_map/ppermute | solution.py:283
  439.2 7.2 collective-permute-done.21
  449.0 9.8 %collective-permute-done.22 = bf16[64,2048]{1,0:T(8,128)(2,1)S(1)} collective-permute-done((bf16[64,2048]{1,0:T(8,128)(2,1)S(1)}, bf16[64,2048]{1,0:T(8,128)(2,1)S(1)}, u32[]{:S(2)}, u32[]{:S(2)}) %collective-permute-start.22) | collective-permute-done | bytes 262176 | tf_op jit(solution)/shard_map/ppermute | solution.py:283
  459.7 47.3 %collective-permute-done.34 = bf16[512,3072]{1,0:T(8,128)(2,1)} collective-permute-done((bf16[512,3072]{1,0:T(8,128)(2,1)}, bf16[512,3072]{1,0:T(8,128)(2,1)}, u32[]{:S(2)}, u32[]{:S(2)}) %collective-permute-start.34) | collective-permute-done | bytes 3145760 | tf_op jit(solution)/shard_map/ppermute | solution.py:287
  513.3 32.0 %collective-permute-done.35 = bf16[256,3072]{1,0:T(8,128)(2,1)S(1)} collective-permute-done((bf16[256,3072]{1,0:T(8,128)(2,1)S(1)}, bf16[256,3072]{1,0:T(8,128)(2,1)S(1)}, u32[]{:S(2)}, u32[]{:S(2)}) %collective-permute-start.35) | collective-permute-done | bytes 1572896 | tf_op jit(solution)/shard_map/ppermute | solution.py:283
  546.3 16.3 %collective-permute-done.36 = bf16[128,3072]{1,0:T(8,128)(2,1)S(1)} collective-permute-done((bf16[128,3072]{1,0:T(8,128)(2,1)S(1)}, bf16[128,3072]{1,0:T(8,128)(2,1)S(1)}, u32[]{:S(2)}, u32[]{:S(2)}) %collective-permute-start.36) | collective-permute-done | bytes 786464 | tf_op jit(solution)/shard_map/ppermute | solution.py:283
  567.4 10.2 %collective-permute-done.37 = bf16[64,3072]{1,0:T(8,128)(2,1)S(1)} collective-permute-done((bf16[64,3072]{1,0:T(8,128)(2,1)S(1)}, bf16[64,3072]{1,0:T(8,128)(2,1)S(1)}, u32[]{:S(2)}, u32[]{:S(2)}) %collective-permute-start.37) | collective-permute-done | bytes 393248 | tf_op jit(solution)/shard_map/ppermute | solution.py:283
  588.3 61.5 %collective-permute-done.28 = bf16[256,3840]{1,0:T(8,128)(2,1)S(1)} collective-permute-done((bf16[256,3840]{1,0:T(8,128)(2,1)S(1)}, bf16[256,3840]{1,0:T(8,128)(2,1)S(1)}, u32[]{:S(2)}, u32[]{:S(2)}) %collective-permute-start.28) | collective-permute-done | bytes 1966112 | tf_op jit(solution)/shard_map/ppermute | solution.py:283
  650.4 37.6 %collective-permute-done.24 = bf16[256,3840]{1,0:T(8,128)(2,1)S(1)} collective-permute-done((bf16[256,3840]{1,0:T(8,128)(2,1)S(1)}, bf16[256,3840]{1,0:T(8,128)(2,1)S(1)}, u32[]{:S(2)}, u32[]{:S(2)}) %collective-permute-start.24) | collective-permute-done | bytes 1966112 | tf_op jit(solution)/shard_map/ppermute | solution.py:283
  688.7 30.1 %collective-permute-done.25 = bf16[128,3840]{1,0:T(8,128)(2,1)S(1)} collective-permute-done((bf16[128,3840]{1,0:T(8,128)(2,1)S(1)}, bf16[128,3840]{1,0:T(8,128)(2,1)S(1)}, u32[]{:S(2)}, u32[]{:S(2)}) %collective-permute-start.25) | collective-permute-done | bytes 983072 | tf_op jit(solution)/shard_map/ppermute | solution.py:283
  719.5 21.8 %collective-permute-done.26 = bf16[64,3840]{1,0:T(8,128)(2,1)S(1)} collective-permute-done((bf16[64,3840]{1,0:T(8,128)(2,1)S(1)}, bf16[64,3840]{1,0:T(8,128)(2,1)S(1)}, u32[]{:S(2)}, u32[]{:S(2)}) %collective-permute-start.26) | collective-permute-done | bytes 491552 | tf_op jit(solution)/shard_map/ppermute | solution.py:283
  742.5 6.4 fusion.53
  748.9 5.5 fusion.9
  773.8 5.5 slice_convert_fusion
  779.2 6.6 copy.55
  785.9 6.6 copy.56
  803.9 8.2 all-gather.15.cloned.1.call-done.grads
  815.3 6.0 shard_map.182
  (298 shorter events, 182.8 us)
Async XLA Ops:
  7.2 148.7 %all-gather.7.cloned.1.call-start = ((), (), s32[]{:S(2)}) async-start(), calls=%async_computation | async-start | bytes 3342336 | tf_op jit(solution)/shard_map/all_gather | solution.py:369
  26.2 149.2 %all-gather.9.cloned.1.call-start = ((), (), s32[]{:S(2)}) async-start(), calls=%async_computation.1 | async-start | bytes 1114112 | tf_op jit(solution)/shard_map/all_gather | solution.py:369
  26.3 92.5 %collective-permute-start.1 = (f32[3,512]{1,0:T(4,128)S(1)}, f32[3,512]{1,0:T(4,128)S(1)}, u32[]{:S(2)}, u32[]{:S(2)}) collective-permute-start(f32[3,512]{1,0:T(4,128)S(1)} %copy-done.50), channel_id=1, source_target_pairs={{0,1},{1,0},{2,3},{3,2},{4,5},{5,4},{6,7},{7,6},{8,9},{9,8},{10,11... | collective-permute-start | bytes 18440 | tf_op jit(solution)/shard_map/ppermute | solution.py:287
  40.4 26.5 %collective-permute-start.8 = (bf16[512,1024]{1,0:T(8,128)(2,1)}, bf16[512,1024]{1,0:T(8,128)(2,1)}, u32[]{:S(2)}, u32[]{:S(2)}) collective-permute-start(bf16[512,1024]{1,0:T(8,128)(2,1)} %get-tuple-element.38), channel_id=1, source_target_pairs={{0,1},{1,0},{2,3},{3,2},{4,5},{5,4},{6,7},{7,6},{8,9},{9,8},{10,11... | collective-permute-start | bytes 3145736 | tf_op jit(solution)/shard_map/ppermute | solution.py:287
  46.8 202.2 %all-gather.11.cloned.1.call-start = ((), (), s32[]{:S(2)}) async-start(), calls=%async_computation.2 | async-start | bytes 5013504 | tf_op jit(solution)/shard_map/all_gather | solution.py:369
  46.9 42.5 %collective-permute-start.10 = (bf16[512,1024]{1,0:T(8,128)(2,1)}, bf16[512,1024]{1,0:T(8,128)(2,1)}, u32[]{:S(2)}, u32[]{:S(2)}) collective-permute-start(bf16[512,1024]{1,0:T(8,128)(2,1)} %get-tuple-element.39), channel_id=1, source_target_pairs={{0,1},{1,0},{2,3},{3,2},{4,5},{5,4},{6,7},{7,6},{8,9},{9,8},{10,11... | collective-permute-start | bytes 3145736 | tf_op jit(solution)/shard_map/ppermute | solution.py:287
  51.5 65.9 %collective-permute-start.4 = (bf16[512,1280]{1,0:T(8,128)(2,1)S(1)}, bf16[512,1280]{1,0:T(8,128)(2,1)}, u32[]{:S(2)}, u32[]{:S(2)}) collective-permute-start(bf16[512,1280]{1,0:T(8,128)(2,1)S(1)} %get-tuple-element.36), channel_id=1, source_target_pairs={{0,1},{1,0},{2,3},{3,2},{4,5},{5,4},{6,7},{7,6},{8,9},{9,8},{10,11... | collective-permute-start | bytes 3932168 | tf_op jit(solution)/shard_map/ppermute | solution.py:287
  52.1 90.5 %collective-permute-start.6 = (bf16[512,1280]{1,0:T(8,128)(2,1)}, bf16[512,1280]{1,0:T(8,128)(2,1)}, u32[]{:S(2)}, u32[]{:S(2)}) collective-permute-start(bf16[512,1280]{1,0:T(8,128)(2,1)} %get-tuple-element.37), channel_id=1, source_target_pairs={{0,1},{1,0},{2,3},{3,2},{4,5},{5,4},{6,7},{7,6},{8,9},{9,8},{10,11... | collective-permute-start | bytes 3932168 | tf_op jit(solution)/shard_map/ppermute | solution.py:287
  66.9 75.8 %collective-permute-start.9 = (bf16[512,1024]{1,0:T(8,128)(2,1)}, bf16[512,1024]{1,0:T(8,128)(2,1)}, u32[]{:S(2)}, u32[]{:S(2)}) collective-permute-start(bf16[512,1024]{1,0:T(8,128)(2,1)} %collective-permute-done.8), channel_id=1, source_target_pairs={{0,2},{2,0},{4,6},{6,4},{8,10},{10,8},{12,14},{14,12},{16,18},{18,... | collective-permute-start | bytes 3145736 | tf_op jit(solution)/shard_map/ppermute | solution.py:283
  89.3 55.0 %collective-permute-start.11 = (bf16[512,1024]{1,0:T(8,128)(2,1)}, bf16[512,1024]{1,0:T(8,128)(2,1)}, u32[]{:S(2)}, u32[]{:S(2)}) collective-permute-start(bf16[512,1024]{1,0:T(8,128)(2,1)} %collective-permute-done.10), channel_id=1, source_target_pairs={{0,2},{2,0},{4,6},{6,4},{8,10},{10,8},{12,14},{14,12},{16,18},{18,... | collective-permute-start | bytes 3145736 | tf_op jit(solution)/shard_map/ppermute | solution.py:283
  117.4 31.7 %collective-permute-start.5 = (bf16[512,1280]{1,0:T(8,128)(2,1)}, bf16[512,1280]{1,0:T(8,128)(2,1)}, u32[]{:S(2)}, u32[]{:S(2)}) collective-permute-start(bf16[512,1280]{1,0:T(8,128)(2,1)} %collective-permute-done.4), channel_id=1, source_target_pairs={{0,2},{2,0},{4,6},{6,4},{8,10},{10,8},{12,14},{14,12},{16,18},{18,... | collective-permute-start | bytes 3932168 | tf_op jit(solution)/shard_map/ppermute | solution.py:283
  118.8 655.0 %all-gather.13.cloned.1.call-start = ((), (), s32[]{:S(2)}) async-start(), calls=%async_computation.3 | async-start | bytes 4456448 | tf_op jit(solution)/shard_map/all_gather | solution.py:369
  360.1 47.8 %collective-permute-start.19 = (bf16[512,2048]{1,0:T(8,128)(2,1)S(1)}, bf16[512,2048]{1,0:T(8,128)(2,1)S(1)}, u32[]{:S(2)}, u32[]{:S(2)}) collective-permute-start(bf16[512,2048]{1,0:T(8,128)(2,1)S(1)} %add_convert_fusion.1), channel_id=1, source_target_pairs={{0,1},{1,0},{2,3},{3,2},{4,5},{5,4},{6,7},{7,6},{8,9},{9,8},{10,11... | collective-permute-start | bytes 6291464 | tf_op jit(solution)/shard_map/ppermute | solution.py:287
  361.2 74.4 %collective-permute-start.33 = (bf16[512,3072]{1,0:T(8,128)(2,1)S(1)}, bf16[512,3072]{1,0:T(8,128)(2,1)S(1)}, u32[]{:S(2)}, u32[]{:S(2)}) collective-permute-start(bf16[512,3072]{1,0:T(8,128)(2,1)S(1)} %copy-done.56), channel_id=1, source_target_pairs={{0,2},{2,0},{4,6},{6,4},{8,10},{10,8},{12,14},{14,12},{16,18},{18,... | collective-permute-start | bytes 9437192 | tf_op jit(solution)/shard_map/ppermute | solution.py:283
  409.1 24.5 %collective-permute-start.20 = (bf16[256,2048]{1,0:T(8,128)(2,1)S(1)}, bf16[256,2048]{1,0:T(8,128)(2,1)S(1)}, u32[]{:S(2)}, u32[]{:S(2)}) collective-permute-start(bf16[256,2048]{1,0:T(8,128)(2,1)S(1)} %get-tuple-element.119), channel_id=1, source_target_pairs={{0,4},{2,6},{4,0},{6,2},{8,12},{10,14},{12,8},{14,10},{16,20},{18,... | collective-permute-start | bytes 3145736 | tf_op jit(solution)/shard_map/ppermute | solution.py:283
  410.8 49.0 %collective-permute-start.32 = (bf16[512,3072]{1,0:T(8,128)(2,1)}, bf16[512,3072]{1,0:T(8,128)(2,1)}, u32[]{:S(2)}, u32[]{:S(2)}) collective-permute-start(bf16[512,3072]{1,0:T(8,128)(2,1)} %get-tuple-element.53), channel_id=1, source_target_pairs={{0,2},{2,0},{4,6},{6,4},{8,10},{10,8},{12,14},{14,12},{16,18},{18,... | collective-permute-start | bytes 9437192 | tf_op jit(solution)/shard_map/ppermute | solution.py:283
  438.5 68.5 %collective-permute-start.34 = (bf16[512,3072]{1,0:T(8,128)(2,1)}, bf16[512,3072]{1,0:T(8,128)(2,1)}, u32[]{:S(2)}, u32[]{:S(2)}) collective-permute-start(bf16[512,3072]{1,0:T(8,128)(2,1)} %add_convert_fusion), channel_id=1, source_target_pairs={{0,1},{1,0},{2,3},{3,2},{4,5},{5,4},{6,7},{7,6},{8,9},{9,8},{10,11... | collective-permute-start | bytes 9437192 | tf_op jit(solution)/shard_map/ppermute | solution.py:287
  446.4 12.4 %collective-permute-start.22 = (bf16[64,2048]{1,0:T(8,128)(2,1)S(1)}, bf16[64,2048]{1,0:T(8,128)(2,1)S(1)}, u32[]{:S(2)}, u32[]{:S(2)}) collective-permute-start(bf16[64,2048]{1,0:T(8,128)(2,1)S(1)} %add_convert_fusion.30), channel_id=1, source_target_pairs={{0,16},{2,18},{4,20},{6,22},{8,24},{10,26},{12,28},{14,30},{16,0},... | collective-permute-start | bytes 786440 | tf_op jit(solution)/shard_map/ppermute | solution.py:283
  459.7 336.1 %all-gather.17.cloned.1.call-start = ((), (), s32[]{:S(2)}) async-start(), calls=%async_computation.5 | async-start | bytes 6684672 | tf_op jit(solution)/shard_map/all_gather | solution.py:369
  511.7 33.6 %collective-permute-start.35 = (bf16[256,3072]{1,0:T(8,128)(2,1)S(1)}, bf16[256,3072]{1,0:T(8,128)(2,1)S(1)}, u32[]{:S(2)}, u32[]{:S(2)}) collective-permute-start(bf16[256,3072]{1,0:T(8,128)(2,1)S(1)} %get-tuple-element.113), channel_id=1, source_target_pairs={{0,4},{2,6},{4,0},{6,2},{8,12},{10,14},{12,8},{14,10},{16,20},{18,... | collective-permute-start | bytes 4718600 | tf_op jit(solution)/shard_map/ppermute | solution.py:283
  545.9 16.8 %collective-permute-start.36 = (bf16[128,3072]{1,0:T(8,128)(2,1)S(1)}, bf16[128,3072]{1,0:T(8,128)(2,1)S(1)}, u32[]{:S(2)}, u32[]{:S(2)}) collective-permute-start(bf16[128,3072]{1,0:T(8,128)(2,1)S(1)} %get-tuple-element.127), channel_id=1, source_target_pairs={{0,8},{2,10},{4,12},{6,14},{8,0},{10,2},{12,4},{14,6},{16,24},{18,... | collective-permute-start | bytes 2359304 | tf_op jit(solution)/shard_map/ppermute | solution.py:283
  546.3 32.2 %collective-permute-start.27 = (bf16[512,3840]{1,0:T(8,128)(2,1)}, bf16[512,3840]{1,0:T(8,128)(2,1)}, u32[]{:S(2)}, u32[]{:S(2)}) collective-permute-start(bf16[512,3840]{1,0:T(8,128)(2,1)} %get-tuple-element.51), channel_id=1, source_target_pairs={{0,2},{2,0},{4,6},{6,4},{8,10},{10,8},{12,14},{14,12},{16,18},{18,... | collective-permute-start | bytes 11796488 | tf_op jit(solution)/shard_map/ppermute | solution.py:283
  562.7 14.9 %collective-permute-start.37 = (bf16[64,3072]{1,0:T(8,128)(2,1)S(1)}, bf16[64,3072]{1,0:T(8,128)(2,1)S(1)}, u32[]{:S(2)}, u32[]{:S(2)}) collective-permute-start(bf16[64,3072]{1,0:T(8,128)(2,1)S(1)} %add_convert_fusion.27), channel_id=1, source_target_pairs={{0,16},{2,18},{4,20},{6,22},{8,24},{10,26},{12,28},{14,30},{16,0},... | collective-permute-start | bytes 1179656 | tf_op jit(solution)/shard_map/ppermute | solution.py:283
  567.4 17.3 %collective-permute-start.23 = (bf16[512,3840]{1,0:T(8,128)(2,1)}, bf16[512,3840]{1,0:T(8,128)(2,1)}, u32[]{:S(2)}, u32[]{:S(2)}) collective-permute-start(bf16[512,3840]{1,0:T(8,128)(2,1)} %get-tuple-element.49), channel_id=1, source_target_pairs={{0,2},{2,0},{4,6},{6,4},{8,10},{10,8},{12,14},{14,12},{16,18},{18,... | collective-permute-start | bytes 11796488 | tf_op jit(solution)/shard_map/ppermute | solution.py:283
  578.5 233.6 %all-gather.15.cloned.1.call-start = ((), (), s32[]{:S(2)}) async-start(), calls=%async_computation.4 | async-start | bytes 8355840 | tf_op jit(solution)/shard_map/all_gather | solution.py:369
  582.9 66.9 %collective-permute-start.28 = (bf16[256,3840]{1,0:T(8,128)(2,1)S(1)}, bf16[256,3840]{1,0:T(8,128)(2,1)S(1)}, u32[]{:S(2)}, u32[]{:S(2)}) collective-permute-start(bf16[256,3840]{1,0:T(8,128)(2,1)S(1)} %get-tuple-element.117), channel_id=1, source_target_pairs={{0,4},{2,6},{4,0},{6,2},{8,12},{10,14},{12,8},{14,10},{16,20},{18,... | collective-permute-start | bytes 5898248 | tf_op jit(solution)/shard_map/ppermute | solution.py:283
  588.1 99.9 %collective-permute-start.24 = (bf16[256,3840]{1,0:T(8,128)(2,1)S(1)}, bf16[256,3840]{1,0:T(8,128)(2,1)S(1)}, u32[]{:S(2)}, u32[]{:S(2)}) collective-permute-start(bf16[256,3840]{1,0:T(8,128)(2,1)S(1)} %get-tuple-element.115), channel_id=1, source_target_pairs={{0,4},{2,6},{4,0},{6,2},{8,12},{10,14},{12,8},{14,10},{16,20},{18,... | collective-permute-start | bytes 5898248 | tf_op jit(solution)/shard_map/ppermute | solution.py:283
  650.3 38.2 %collective-permute-start.29 = (bf16[128,3840]{1,0:T(8,128)(2,1)S(1)}, bf16[128,3840]{1,0:T(8,128)(2,1)S(1)}, u32[]{:S(2)}, u32[]{:S(2)}) collective-permute-start(bf16[128,3840]{1,0:T(8,128)(2,1)S(1)} %get-tuple-element.125), channel_id=1, source_target_pairs={{0,8},{2,10},{4,12},{6,14},{8,0},{10,2},{12,4},{14,6},{16,24},{18,... | collective-permute-start | bytes 2949128 | tf_op jit(solution)/shard_map/ppermute | solution.py:283
  688.4 30.3 %collective-permute-start.25 = (bf16[128,3840]{1,0:T(8,128)(2,1)S(1)}, bf16[128,3840]{1,0:T(8,128)(2,1)S(1)}, u32[]{:S(2)}, u32[]{:S(2)}) collective-permute-start(bf16[128,3840]{1,0:T(8,128)(2,1)S(1)} %get-tuple-element.123), channel_id=1, source_target_pairs={{0,8},{2,10},{4,12},{6,14},{8,0},{10,2},{12,4},{14,6},{16,24},{18,... | collective-permute-start | bytes 2949128 | tf_op jit(solution)/shard_map/ppermute | solution.py:283
  688.6 30.3 %collective-permute-start.30 = (bf16[64,3840]{1,0:T(8,128)(2,1)S(1)}, bf16[64,3840]{1,0:T(8,128)(2,1)S(1)}, u32[]{:S(2)}, u32[]{:S(2)}) collective-permute-start(bf16[64,3840]{1,0:T(8,128)(2,1)S(1)} %add_convert_fusion.21), channel_id=1, source_target_pairs={{0,16},{2,18},{4,20},{6,22},{8,24},{10,26},{12,28},{14,30},{16,0},... | collective-permute-start | bytes 1474568 | tf_op jit(solution)/shard_map/ppermute | solution.py:283
  718.9 22.4 %collective-permute-start.26 = (bf16[64,3840]{1,0:T(8,128)(2,1)S(1)}, bf16[64,3840]{1,0:T(8,128)(2,1)S(1)}, u32[]{:S(2)}, u32[]{:S(2)}) collective-permute-start(bf16[64,3840]{1,0:T(8,128)(2,1)S(1)} %add_convert_fusion.24), channel_id=1, source_target_pairs={{0,16},{2,18},{4,20},{6,22},{8,24},{10,26},{12,28},{14,30},{16,0},... | collective-permute-start | bytes 1474568 | tf_op jit(solution)/shard_map/ppermute | solution.py:283
  719.2 22.1 %collective-permute-start.31 = (bf16[64,3840]{1,0:T(8,128)(2,1)S(1)}, bf16[64,3840]{1,0:T(8,128)(2,1)S(1)}, u32[]{:S(2)}, u32[]{:S(2)}) collective-permute-start(bf16[64,3840]{1,0:T(8,128)(2,1)S(1)} %add_convert_fusion.20), channel_id=1, source_target_pairs={{0,1},{1,0},{2,3},{3,2},{4,5},{5,4},{6,7},{7,6},{8,9},{9,8},{10,11... | collective-permute-start | bytes 1474568 | tf_op jit(solution)/shard_map/ppermute | solution.py:287
  (77 other events, 989.8 us)
Sparse Core Ops, SparseCore 0:
  26.4 46.9 all-gather.6
  76.0 36.7 all-gather.8
  118.9 53.8 all-gather.10
  459.8 50.8 all-gather.12
  578.6 84.4 all-gather.16
  742.5 69.5 all-gather.14

commit v2 on v1

--- a/solution.py
+++ b/solution.py
@@ -149,7 +149,7 @@
 
 WIDE = 256
 ROW_TILE = 512
-GROUPS = (4, 5)
+GROUPS = (3, 3, 3)
 MIB = 1024 * 1024
 
 
@@ -159,7 +159,7 @@
     return (
         tensor == 2
         and dp & (dp - 1) == 0
-        and 2 <= dp <= 16
+        and 4 <= dp <= 16
         and tokens.shape[0] % LEN == 0
         and tokens.shape[1] == 1024
         and proj_in.shape[2] % 128 == 0
@@ -167,21 +167,14 @@
     )
 
 
-def ffn_body(first, *refs):
-    if first:
-        h, ht, e, et, wg, wu, wd, branch, grad_h, keep, send, zs, gg, gu = refs
-    else:
-        h, ht, e, et, wg, wu, wd, branch_in, grad_in, branch, grad_h, keep, send, zs, gg, gu = refs
+def ffn_body(h, ht, e, et, wg, wu, wd, branch, grad_h, keep, send, zs, gg, gu, branch_sum, grad_sum):
     rows, half, wide = h.shape[0], keep.shape[0], wg.shape[1]
-
-    @pl.when(pl.program_id(0) == 0)
+    step = pl.program_id(0)
+
+    @pl.when(step == 0)
     def _():
-        if first:
-            branch[...] = jnp.zeros_like(branch)
-            grad_h[...] = jnp.zeros_like(grad_h)
-        else:
-            branch[...] = branch_in[...]
-            grad_h[...] = grad_in[...]
+        branch_sum[...] = jnp.zeros_like(branch_sum)
+        grad_sum[...] = jnp.zeros_like(grad_sum)
 
     for start in range(0, rows, ROW_TILE):
         r = pl.ds(start, ROW_TILE)
@@ -196,70 +189,79 @@
         zs[r, :] = hidden
         gg[r, :] = grad_gate
         gu[r, :] = grad_up
-        branch[r, :] += times_rows(hidden, wd[...])
-        grad_h[r, :] += right_outer(grad_gate, wg[...]) + right_outer(grad_up, wu[...])
+        branch_sum[r, :] += times_rows(hidden, wd[...])
+        grad_sum[r, :] += right_outer(grad_gate, wg[...]) + right_outer(grad_up, wu[...])
     for out, base in ((keep, 0), (send, half)):
         a = ht[pl.ds(base, half), :]
         out[:, 0:wide] = times_rows(a, gg[...]).astype(jnp.bfloat16)
         out[:, wide : 2 * wide] = times_rows(a, gu[...]).astype(jnp.bfloat16)
         out[:, 2 * wide : 3 * wide] = times_rows(et[pl.ds(base, half), :], zs[...]).astype(jnp.bfloat16)
 
-
-def ffn_part(h, ht, e, et, wg, wu, wd, sums, gate_at, down_at, count):
+    @pl.when(step == pl.num_programs(0) - 1)
+    def _():
+        branch[...] = branch_sum[...].astype(jnp.bfloat16)
+        grad_h[...] = grad_sum[...].astype(jnp.bfloat16)
+
+
+def ffn_part(h, ht, e, et, wg, wu, wd, gate_at, up_at, down_at, count):
     rows, width = h.shape
-    first = sums is None
 
     def whole(shape):
         return pl.BlockSpec(shape, lambda j: (0, 0), pipeline_mode=pl.Buffered(1))
 
-    in_specs = [
-        whole((rows, width)),
-        whole((width, rows)),
-        whole((rows, width)),
-        whole((width, rows)),
-        pl.BlockSpec((width, WIDE), lambda j: (0, gate_at + j)),
-        pl.BlockSpec((width, WIDE), lambda j: (0, gate_at + j)),
-        pl.BlockSpec((WIDE, width), lambda j: (down_at + j, 0)),
-    ]
-    args = [h, ht, e, et, wg, wu, wd]
-    if not first:
-        in_specs += [whole((rows, width))] * 2
-        args += list(sums)
     branch, grad_h, keep, send = pl.pallas_call(
-        functools.partial(ffn_body, first),
+        ffn_body,
         grid=(count,),
-        in_specs=in_specs,
+        in_specs=[
+            whole((rows, width)),
+            whole((width, rows)),
+            whole((rows, width)),
+            whole((width, rows)),
+            pl.BlockSpec((width, WIDE), lambda j: (0, gate_at + j)),
+            pl.BlockSpec((width, WIDE), lambda j: (0, up_at + j)),
+            pl.BlockSpec((WIDE, width), lambda j: (down_at + j, 0)),
+        ],
         out_specs=[pl.BlockSpec((rows, width), lambda j: (0, 0))] * 2
         + [pl.BlockSpec((width // 2, 3 * WIDE), lambda j: (0, j))] * 2,
-        out_shape=[jax.ShapeDtypeStruct((rows, width), jnp.float32)] * 2
+        out_shape=[jax.ShapeDtypeStruct((rows, width), jnp.bfloat16)] * 2
         + [jax.ShapeDtypeStruct((width // 2, 3 * WIDE * count), jnp.bfloat16)] * 2,
-        scratch_shapes=[pltpu.VMEM((rows, WIDE), jnp.bfloat16)] * 3,
-        input_output_aliases={} if first else {7: 0, 8: 1},
+        scratch_shapes=[pltpu.VMEM((rows, WIDE), jnp.bfloat16)] * 3
+        + [pltpu.VMEM((rows, width), jnp.float32)] * 2,
         compiler_params=pltpu.CompilerParams(vmem_limit_bytes=56 * MIB),
         cost_estimate=pl.CostEstimate(
-            flops=20 * rows * width * WIDE * count,
-            bytes_accessed=12 * width * WIDE * count + 16 * rows * width,
-            transcendentals=rows * WIDE * count,
+            flops=8 * rows * width * WIDE * count, bytes_accessed=MIB, transcendentals=0
         ),
-    )(*args)
+    )(h, ht, e, et, wg, wu, wd)
     return (branch, grad_h), (keep, send)
 
 
-def ffn_final_body(grads, *refs):
+def ffn_final_body(restored, *refs):
     gate, up, down = refs[-3:]
-    gate[...] = grads[:, 0:WIDE].astype(jnp.float32)
-    up[...] = grads[:, WIDE : 2 * WIDE].astype(jnp.float32)
-    down[...] = grads[:, 2 * WIDE : 3 * WIDE].astype(jnp.float32).T
-
-
-def ffn_final(grads, totals, at, columns):
-    width = grads.shape[0]
-    count = grads.shape[1] // (3 * WIDE)
+    cuts = [slice(k * WIDE, (k + 1) * WIDE) for k in range(3)]
+    if restored:
+        grads = refs[0]
+        gate[...] = grads[:, cuts[0]].astype(jnp.float32)
+        up[...] = grads[:, cuts[1]].astype(jnp.float32)
+        down[...] = grads[:, cuts[2]].astype(jnp.float32).T
+        return
+    own, other, restore, order = refs[:4]
+    half = own.shape[0]
+    gate[...] = times_rows(restore[:, :half], own[:, cuts[0]]) + times_rows(restore[:, half:], other[:, cuts[0]])
+    up[...] = times_rows(restore[:, :half], own[:, cuts[1]]) + times_rows(restore[:, half:], other[:, cuts[1]])
+    down[...] = left_outer(own[:, cuts[2]], order[:half, :]) + left_outer(other[:, cuts[2]], order[half:, :])
+
+
+def ffn_final(grads, totals, at, columns, orders):
+    restored = len(grads) == 1
+    width = orders[0].shape[0]
+    count = grads[0].shape[1] // (3 * WIDE)
     old = [] if totals is None else list(totals)
+    new = list(grads) if restored else list(grads) + list(orders)
     return pl.pallas_call(
-        ffn_final_body,
+        functools.partial(ffn_final_body, restored),
         grid=(count,),
-        in_specs=[pl.BlockSpec((width, 3 * WIDE), lambda j: (0, j))]
+        in_specs=[pl.BlockSpec((g.shape[0], 3 * WIDE), lambda j: (0, j)) for g in grads]
+        + [pl.BlockSpec(g.shape, lambda j: (0, 0)) for g in new[len(grads) :]]
         + [pl.BlockSpec(memory_space=pl.ANY)] * len(old),
         out_specs=[
             pl.BlockSpec((width, WIDE), lambda j: (0, at + j)),
@@ -271,12 +273,10 @@
             jax.ShapeDtypeStruct((width, columns), jnp.float32),
             jax.ShapeDtypeStruct((columns, width), jnp.float32),
         ],
-        input_output_aliases={1 + i: i for i in range(len(old))},
+        input_output_aliases={len(new) + i: i for i in range(len(old))},
         compiler_params=pltpu.CompilerParams(vmem_limit_bytes=40 * MIB),
-        cost_estimate=pl.CostEstimate(
-            flops=0, bytes_accessed=18 * width * WIDE * count, transcendentals=0
-        ),
-    )(grads, *old)
+        cost_estimate=pl.CostEstimate(flops=MIB, bytes_accessed=MIB, transcendentals=0),
+    )(*new, *old)
 
 
 def swap(values, dp, bit):
@@ -284,7 +284,7 @@
 
 
 def cross(values):
-    return lax.ppermute(values, "tensor", [(0, 1), (1, 0)])
+    return jax.tree.map(lambda v: lax.ppermute(v, "tensor", [(0, 1), (1, 0)]), values)
 
 
 def add(*terms):
@@ -294,12 +294,83 @@
     return total.astype(terms[0].dtype)
 
 
-def halve(terms, dp, bits):
-    for bit in bits:
-        half = terms[0].shape[0] // 2
-        got = swap(add(*[t[half:] for t in terms]), dp, bit)
-        terms = [add(*[t[:half] for t in terms]), got]
-    return add(*terms)
+def after(values, *others):
+    return lax.optimization_barrier((values, others))[0]
+
+
+class Chain:
+    def __init__(self, dp, terms, bit=0):
+        self.dp, self.bit, self.terms = dp, bit, terms
+
+    def halve(self, *others):
+        half = self.terms[0].shape[0] // 2
+        total = after(add(*[t[half:] for t in self.terms]), *others)
+        self.bit += 1
+        self.terms = [add(*[t[:half] for t in self.terms]), swap(total, self.dp, self.bit)]
+        return total
+
+    def total(self):
+        return add(*self.terms)
+
+    def settle(self, *others):
+        total = after(self.total(), *others)
+        self.terms = [total]
+        return total
+
+    def take(self, other, *others):
+        total = after(other.total(), *others)
+        self.terms = self.terms + [cross(total)]
+        return total
+
+    def take_cut(self, other, cut, *others):
+        total = after(add(*[t[:, cut] for t in other.terms]), *others)
+        part = Chain(self.dp, [t[:, cut] for t in self.terms] + [cross(total)], self.bit)
+        return part, total
+
+    def gather(self, *others):
+        total = after(self.total(), *others)
+        self.result = (lax.all_gather(total, "dp", axis=0, tiled=True),)
+        return total
+
+    def collect(self, *others):
+        total = after(jnp.concatenate(self.terms, 0) if self.bit < 0 else self.total(), *others)
+        self.bit = ~self.bit if self.bit >= 0 else self.bit
+        self.terms = [total, swap(total, self.dp, ~self.bit)]
+        self.bit += 1
+        self.result = tuple(self.terms)
+        return total
+
+
+def mixer_final_body(own1, other1, own2, other2, restore, order, grad_in, grad_out):
+    channels = grad_in.shape[2]
+    half = own1.shape[0]
+    low, high = restore[:, :half], restore[:, half:]
+    for k, (own, other, at) in enumerate(((own1, other1, 0), (own1, other1, 1), (own2, other2, 0))):
+        cut = slice(at * channels, (at + 1) * channels)
+        grad_in[k] = times_rows(low, own[:, cut]) + times_rows(high, other[:, cut])
+    cut = slice(channels, 2 * channels)
+    grad_out[...] = left_outer(own2[:, cut], order[:half, :]) + left_outer(other2[:, cut], order[half:, :])
+
+
+def mixer_final(first, second, orders):
+    half, pair = first[0].shape
+    width, channels, rows = 2 * half, pair // 2, 256
+    return pl.pallas_call(
+        mixer_final_body,
+        grid=(width // rows,),
+        in_specs=[pl.BlockSpec((half, pair), lambda j: (0, 0))] * 4
+        + [pl.BlockSpec((rows, width), lambda j: (j, 0)), pl.BlockSpec((width, rows), lambda j: (0, j))],
+        out_specs=[
+            pl.BlockSpec((3, rows, channels), lambda j: (0, j, 0)),
+            pl.BlockSpec((channels, rows), lambda j: (0, j)),
+        ],
+        out_shape=[
+            jax.ShapeDtypeStruct((3, width, channels), jnp.float32),
+            jax.ShapeDtypeStruct((channels, width), jnp.float32),
+        ],
+        compiler_params=pltpu.CompilerParams(vmem_limit_bytes=40 * MIB),
+        cost_estimate=pl.CostEstimate(flops=MIB, bytes_accessed=MIB, transcendentals=0),
+    )(*first, *second, *orders)
 
 
 def block_order(me, dp, width, bits):
@@ -359,44 +430,47 @@
     channels = proj_in.shape[2]
     hidden = w_gate.shape[1]
     bits = tuple(range(dp.bit_length() - 1))
-    flat_in = proj_in.reshape(width, 3 * channels)
-
-    def far_blocks(values):
-        size = values.shape[0] // dp
-        return cross(lax.dynamic_slice_in_dim(values, me * size, size, 0))
 
     def gathered(blocks):
         return lax.all_gather(blocks, "dp", axis=0, tiled=True)
 
-    in_blocks, out_blocks, down_blocks = far_blocks(flat_in), far_blocks(proj_out), far_blocks(w_down)
+    half = width // 2
+    def my_rows(values):
+        size = values.shape[0] // dp
+        return lax.dynamic_slice_in_dim(values, me * size, size, 0)
+
+    in_blocks = cross(my_rows(proj_in).reshape(width // dp, 3 * channels))
+    out_half = cross(lax.dynamic_slice_in_dim(proj_out, core * (channels // 2), channels // 2, 0))
     taps_far = cross(taps)
     flat_in_far = gathered(in_blocks)
-    proj_out_far = gathered(out_blocks)
-    w_down_far = gathered(down_blocks)
-
-    def far_columns(values, at, count, after):
-        part = lax.dynamic_slice(values, (core * (width // 2), at), (width // 2, count))
-        part, _ = lax.optimization_barrier((part, after))
-        mine = cross(part)
+    late = GROUPS[0] * WIDE
+
+    def far_join(mine, axis):
         other = swap(mine, dp, 0)
-        return jnp.concatenate([jnp.where(core == 0, mine, other), jnp.where(core == 0, other, mine)], 0)
-
-    far, at, after = [], 0, (in_blocks, out_blocks, down_blocks)
-    for count in GROUPS:
-        gate_far = far_columns(w_gate, at * WIDE, count * WIDE, after)
-        up_far = far_columns(w_up, at * WIDE, count * WIDE, after)
-        far.append((gate_far, up_far))
-        at += count
+        return jnp.concatenate([jnp.where(core == 0, mine, other), jnp.where(core == 0, other, mine)], axis)
+
+    def gate_part(at, count):
+        return jnp.concatenate(
+            [lax.dynamic_slice(w, (core * half, at * WIDE), (half, count * WIDE)) for w in (w_gate, w_up)], 1
+        )
+
+    first_sent = after(
+        (gate_part(0, GROUPS[0]), lax.dynamic_slice(w_down, (core * (late // 2), 0), (late // 2, width))),
+        in_blocks,
+    )
+    first = cross(first_sent)
+    flat_in = after(proj_in, first_sent).reshape(width, 3 * channels)
+    proj_out_far = far_join(out_half, 0)
 
     order = block_order(me, dp, width, bits)
-    cot_t = ordered(order, cotangent)
+    cot_t = ordered(order, after(cotangent, first_sent))
 
     resid_in = tokens.astype(jnp.float32)
     scale_mix = lax.rsqrt(jnp.mean(resid_in * resid_in, axis=-1, keepdims=True) + epsilon)
     unit_mix = resid_in * scale_mix
     normed = (unit_mix * gain_mix).astype(jnp.bfloat16)
-    normed_t = ordered(order, normed)
-    kept = mixer_forward(normed, flat_in, taps)
+    normed_t = ordered(order, after(normed, first_sent))
+    kept = mixer_forward(after(normed, first_sent), flat_in, taps)
     kept_far = mixer_forward(normed, flat_in_far, taps_far)
     mixer = times_rows(kept[-1], proj_out) + times_rows(kept_far[-1], proj_out_far)
     middle = resid_in + mixer
@@ -404,75 +478,138 @@
     unit_ffn = middle * scale_ffn
     normed_mid = (unit_ffn * gain_ffn).astype(jnp.bfloat16)
     normed_mid_t = ordered(order, normed_mid)
-
-    sums, near_grads, far_grads, at = None, [], [], 0
-    for count in GROUPS:
+    first = after(first, middle)
+    rest = (hidden - late) // dp
+    down_blocks = cross(lax.dynamic_slice_in_dim(after(w_down, first), late + me * rest, rest, 0))
+    down_late = gathered(down_blocks)
+
+    def gate_send(index, received):
+        part = after(gate_part(sum(GROUPS[:index]), GROUPS[index]), received)
+        return part, cross(part)
+
+    parts = []
+    received = first
+
+    def far_part(index, gates_far, down_far, down_at, *others):
         sums, grads = ffn_part(
-            normed_mid, normed_mid_t, cotangent, cot_t, w_gate, w_up, w_down, sums, at, at, count
+            after(normed_mid, others),
+            normed_mid_t,
+            cotangent,
+            cot_t,
+            gates_far,
+            gates_far,
+            down_far,
+            0,
+            GROUPS[index],
+            down_at,
+            GROUPS[index],
         )
-        near_grads.append(grads)
-        at += count
-    at = 0
-    for count, (gate_far, up_far) in zip(GROUPS, far):
+        parts.append(sums)
+        return grads
+
+    def near_part(index, *others):
+        at = sum(GROUPS[:index])
         sums, grads = ffn_part(
-            normed_mid, normed_mid_t, cotangent, cot_t, gate_far, up_far, w_down_far, sums, 0, at, count
+            after(normed_mid, others), normed_mid_t, cotangent, cot_t, w_gate, w_up, w_down, at, at, at, GROUPS[index]
         )
-        far_grads.append(grads)
-        at += count
-
-    def reduced(near, far, far_first):
-        near = [near[0], swap(near[1], dp, bits[0])]
-        far = [far[0], swap(far[1], dp, bits[0])]
-        if far_first:
-            return gathered(halve(near + [cross(add(*far))], dp, bits[1:]))
-        return gathered(add(halve(near, dp, bits[1:]), cross(halve(far, dp, bits[1:]))))
-
-    totals, at = None, 0
-    for index, count in enumerate(GROUPS):
-        grads = reduced(near_grads[index], far_grads[index], FAR_FIRST[index])
-        totals = ffn_final(grads, totals, at, hidden)
-        at += count
-    grad_w_gate, grad_w_up, grad_w_down = totals
-
-    branch, grad_mid = sums
-    output = (middle + branch).astype(jnp.bfloat16)
+        parts.append(sums)
+        return grads
+
+    def chain(grads):
+        return Chain(dp, [grads[0], swap(grads[1], dp, 0)])
+
+    gates0, down0 = far_join(first[0], 0), far_join(first[1], 0)
+    sending, second = gate_send(1, (first, down_blocks))
+    grads = far_part(0, gates0, down0, 0, sending, cot_t, normed_t)
+    far0 = chain(grads)
+    sending, third = gate_send(2, second)
+    grads = near_part(0, grads, sending)
+    near0 = chain(grads)
+    gates1 = far_join(second, 0)
+    grads = far_part(1, gates1, down_late, 0, grads, far0.halve(grads))
+    far1 = chain(grads)
+    grads = near_part(1, grads, near0.halve(grads), far0.halve(grads))
+    near1 = chain(grads)
+    gates2 = far_join(after(third, grads), 0)
+    grads = far_part(2, gates2, down_late, GROUPS[1], grads, near1.take(far1, grads), far0.halve(grads), near0.halve(grads))
+    far2 = chain(grads)
+    near1.terms = [add(*near1.terms[:2]), near1.terms[2]]
+    far0.settle(grads)
+    grads = near_part(2, grads, near0.halve(grads), near1.terms[0], far0.terms)
+    near2 = chain(grads)
+    branch = sum(part[0].astype(jnp.float32) for part in parts)
+    grad_mid = sum(part[1].astype(jnp.float32) for part in parts)
+    grad_mid = after(grad_mid, near0.take(far0, grads), near2.take(far2, grads))
+    near2.terms = [after(add(*near2.terms[:2]), grad_mid), near2.terms[2]]
     grad_gain_ffn = jnp.sum(grad_mid * unit_ffn, axis=0)
     grad_middle = cotangent.astype(jnp.float32) + norm_back(grad_mid * gain_ffn, unit_ffn, scale_ffn)
     mixer_cot = grad_middle.astype(jnp.bfloat16)
+    mixer_cot = after(mixer_cot, near1.halve(grad_mid), near2.terms[0])
     mixer_cot_t = ordered(order, mixer_cot)
     grad_taps, grad_proj = mixer_backward(right_outer(mixer_cot, proj_out), kept, taps)
     grad_taps_far, grad_proj_far = mixer_backward(right_outer(mixer_cot, proj_out_far), kept_far, taps_far)
 
     def mixer_grads(grad_proj, gated):
-        def rows(part):
-            return jnp.concatenate(
+        return tuple(
+            jnp.concatenate(
                 [times_rows(normed_t[part], grad_proj), times_rows(mixer_cot_t[part], gated)], 1
             ).astype(jnp.bfloat16)
-
-        return rows(slice(0, width // 2)), rows(slice(width // 2, width))
-
-    grads = reduced(
-        mixer_grads(grad_proj, kept[-1]), mixer_grads(grad_proj_far, kept_far[-1]), FAR_FIRST[-1]
-    )
-    grad_proj_in = grads[:, : 3 * channels].astype(jnp.float32).reshape(width, 3, channels)
-    grad_proj_out = grads[:, 3 * channels :].astype(jnp.float32).T
+            for part in (slice(0, half), slice(half, width))
+        )
+
+    both = (grad_proj, grad_proj_far)
+    both = after(both, near0.gather(both))
+    grads = mixer_grads(both[1], kept_far[-1])
+    far3 = chain(grads)
+    grads = mixer_grads(after(both[0], grads), kept[-1])
+    near3 = chain(grads)
+    near4, token4 = near3.take_cut(far3, slice(0, 2 * channels), grads)
+    near5, token5 = near3.take_cut(far3, slice(2 * channels, 4 * channels), grads)
+    near4.terms = [add(*near4.terms[:2]), near4.terms[2]]
+    near5.terms = [add(*near5.terms[:2]), near5.terms[2]]
+    grad_proj, grad_proj_far = after(both, token4, token5, near4.terms[0], near5.terms[0])
 
     grad_normed = right_outer(grad_proj, flat_in) + right_outer(grad_proj_far, flat_in_far)
     grad_gain_mix = jnp.sum(grad_normed * unit_mix, axis=0)
     grad_tokens = grad_middle + norm_back(grad_normed * gain_mix, unit_mix, scale_mix)
 
+    output = (middle + branch).astype(jnp.bfloat16)
     gains = jnp.concatenate([grad_gain_mix[None], grad_gain_ffn[None]], 0)
-    small = jnp.concatenate([gains[:, :channels], gains[:, channels:], grad_taps], 0)
-    small_far = jnp.concatenate([gains[:, :channels], gains[:, channels:], grad_taps_far], 0)
-    small = small + cross(small_far)
-    for bit in bits:
+    small = jnp.concatenate([gains[:, :channels], gains[:, channels:], grad_taps, grad_taps_far], 0)
+    for bit in (0,) + bits[2:] + (1,):
         small = small + swap(small, dp, bit)
+    small = small[0:7] + cross(jnp.concatenate([small[0:4], small[7:10]], 0))
     gains = jnp.concatenate([small[0:2], small[2:4]], 1)
+    orders = (order.T, order)
+    token = near1.halve(grad_normed)
+    token = near2.halve(token)
+    token = near1.halve(token, grad_tokens, output)
+    token = near4.halve(token)
+    token = near2.halve(token)
+    token = near1.gather(token, near0.result)
+    token = near5.halve(token)
+    token = near4.halve(token)
+    token = near2.halve(token)
+    token = near5.halve(token)
+    token = near4.halve(token)
+    token = near5.halve(token)
+    token = near4.collect(token)
+    totals = ffn_final(after(near0.result, token), None, 0, hidden, orders)
+    token = near5.collect(token, totals[0])
+    token = near2.gather(token, near1.result)
+    totals = ffn_final(near1.result, totals, GROUPS[0], hidden, orders)
+    token = (token, totals[0])
+    for _ in bits[1:]:
+        token = near4.collect(token)
+        token = near5.collect(token)
+    totals = ffn_final(near2.result, totals, sum(GROUPS[:2]), hidden, orders)
+    grad_w_gate, grad_w_up, grad_w_down = totals
+    grad_proj_in, grad_proj_out = mixer_final(near4.result, near5.result, orders)
     return (
         output,
         grad_tokens,
         gains[0],
-        grad_proj_in,
+        grad_proj_in.transpose(1, 0, 2),
         small[4:7],
         grad_proj_out,
         gains[1],
@@ -480,9 +617,6 @@
         grad_w_up,
         grad_w_down,
     )
-
-
-FAR_FIRST = (True, False, True)
 
 
 def solution(mesh):

time: 837 us -> 646 us (0.77)
  waiting for transfers between devices: 452 us -> 208 us
  other arithmetic: 78.3 us -> 110 us
  Pallas kernels: 138 us -> 159 us
  starting transfers between devices: 31.4 us -> 48.4 us
  local copies, waits for them, and re-layouts: 49.5 us -> 37.7 us
    ppermute x12 -> x14, waiting for transfers between devices: 187 us -> 26.3 us  [cross(): lax.ppermute(v, 'tensor', [(0, 1), (1, 0)])]
    ppermute x26 -> x43, waiting for transfers between devices: 256 us -> 170 us  [swap(): return lax.ppermute(values, 'dp', [(i, i ^ 1 << bit) for i in range(dp)])]
    convert_element_type x18 -> x30, other arithmetic: 22.3 us -> 47.2 us  [add(): return total.astype(terms[0].dtype)]
    pallas_call x6 -> x10, Pallas kernels: 138 us -> 159 us  [the longest x6 140 us: ffn_part(): pl.pallas_call(ffn_body, grid=(count,), in_specs=[whole((rows, width)), w...]
    ppermute x26 -> x43, starting transfers between devices: 17.6 us -> 30.3 us  [swap(): return lax.ppermute(values, 'dp', [(i, i ^ 1 << bit) for i in range(dp)])]
    unnamed x133 -> x173, local copies, waits for them, and re-layouts: 30.6 us -> 24.2 us
    ppermute x12 -> x14, starting transfers between devices: 13.4 us -> 17.5 us  [cross(): lax.ppermute(v, 'tensor', [(0, 1), (1, 0)])]
  transfers between devices with their start and end apart: 44 -> 62, of which waited for: 22 -> 23; matrix products, arithmetic and copies ran while one was open for 16% -> 29% of each run, Pallas kernels for 8% -> 24%
where the time goes in v2:
time: 646 us; the launch traced here: 642 us
  waiting for transfers between devices  208 us (32%)
  Pallas kernels  159 us (25%)
  other arithmetic  110 us (17%)
  matrix products  63.8 us (10%)
  starting transfers between devices  48.4 us (7%)
  local copies, waits for them, and re-layouts  37.7 us (6%)
  between operations  15.2 us (2%)
    ppermute x43, waiting for transfers between devices, swap(): return lax.ppermute(values, 'dp', [(i, i ^ 1 << bit) for i in range(dp)])  170 us
    pallas_call x6, Pallas kernels, ffn_part(): pl.pallas_call(ffn_body, grid=(count,), in_specs=[whole((rows, width)), w...  140 us
    convert_element_type x30, other arithmetic, add(): return total.astype(terms[0].dtype)  47.2 us
    dot_general x8, matrix products, right_outer(): lax.dot_general(left, right, (((1,), (1,)), ((), ())), preferred_element_...  37.5 us
    ppermute x43, starting transfers between devices, swap(): return lax.ppermute(values, 'dp', [(i, i ^ 1 << bit) for i in range(dp)])  30.3 us
    ppermute x14, waiting for transfers between devices, cross(): lax.ppermute(v, 'tensor', [(0, 1), (1, 0)])  26.3 us
    dot_general x12, matrix products, times_rows(): return jnp.dot(left, right, preferred_element_type=jnp.float32)  26.3 us
    unnamed x173, local copies, waits for them, and re-layouts  24.2 us
  transfers between devices with their start and end apart: 62, of which 23 were waited for; matrix products, arithmetic and copies ran while one was open for 29% of the time, Pallas kernels for 24%

profile of v2, /device:TPU:0, one launch (start us, length us, event | category | flops | bytes accessed | tf_op | source)
XLA Modules:
  0.0 642.2 jit_solution(15545482238406135033)
XLA Ops:
  31.0 4.8 copy.33
  35.8 4.7 convolution_convert_fusion.6
  40.5 4.8 convolution_convert_fusion.7.et
  53.6 11.4 %all-gather.6.cloned.1.call-done = bf16[1024,1536]{1,0:T(8,128)(2,1)} async-done(((bf16[64,1536]{1,0:T(8,128)(2,1)}), bf16[1024,1536]{1,0:T(8,128)(2,1)}) %all-gather.6.cloned.1.call-update) | async-done | bytes 3145744 | tf_op jit(solution)/shard_map/all_gather | solution.py:435
  65.0 5.9 fusion.79
  88.9 4.9 convolution_convert_fusion.5.ht
  102.3 23.3 %shard_map.177 = (bf16[1024,1024]{1,0:T(8,128)(2,1)}, bf16[1024,1024]{1,0:T(8,128)(2,1)}, bf16[512,2304]{1,0:T(8,128)(2,1)}, bf16[512,2304]{1,0:T(8,128)(2,1)}) custom-call(bf16[1024,1024]{1,0:T(8,128)(2,1)} %copy-done.55, bf16[1024,1024]{1,0:T(8,128)(2,1)} %convolution_convert_fusion.5.ht, bf16[1024,1024]{1,0:T(8,128)(2,1)} %e.11, ...), custom_call_target="tpu_custom_call" | custom-call | flops 6442450944 | bytes 1048576 | tf_op jit(solution)/shard_map/pallas_call | solution.py:212
  130.5 23.8 %shard_map.178 = (bf16[1024,1024]{1,0:T(8,128)(2,1)}, bf16[1024,1024]{1,0:T(8,128)(2,1)}, bf16[512,2304]{1,0:T(8,128)(2,1)}, bf16[512,2304]{1,0:T(8,128)(2,1)}) custom-call(bf16[1024,1024]{1,0:T(8,128)(2,1)} %copy-done.55, bf16[1024,1024]{1,0:T(8,128)(2,1)} %convolution_convert_fusion.5.ht, bf16[1024,1024]{1,0:T(8,128)(2,1)} %e.11, ...), custom_call_target="tpu_custom_call" | custom-call | flops 6442450944 | bytes 1048576 | tf_op jit(solution)/shard_map/pallas_call | solution.py:212
  165.5 20.2 %collective-permute-done.13 = bf16[256,2304]{1,0:T(8,128)(2,1)S(1)} collective-permute-done((bf16[256,2304]{1,0:T(8,128)(2,1)S(1)}, bf16[256,2304]{1,0:T(8,128)(2,1)S(1)}, u32[]{:S(2)}, u32[]{:S(2)}) %collective-permute-start.13) | collective-permute-done | bytes 1179680 | tf_op jit(solution)/shard_map/ppermute | solution.py:283
  187.1 23.2 %shard_map.179 = (bf16[1024,1024]{1,0:T(8,128)(2,1)}, bf16[1024,1024]{1,0:T(8,128)(2,1)}, bf16[512,2304]{1,0:T(8,128)(2,1)}, bf16[512,2304]{1,0:T(8,128)(2,1)}) custom-call(bf16[1024,1024]{1,0:T(8,128)(2,1)} %copy-done.55, bf16[1024,1024]{1,0:T(8,128)(2,1)} %convolution_convert_fusion.5.ht, bf16[1024,1024]{1,0:T(8,128)(2,1)} %e.11, ...), custom_call_target="tpu_custom_call" | custom-call | flops 6442450944 | bytes 1048576 | tf_op jit(solution)/shard_map/pallas_call | solution.py:212
  212.8 23.3 %shard_map.180 = (bf16[1024,1024]{1,0:T(8,128)(2,1)}, bf16[1024,1024]{1,0:T(8,128)(2,1)}, bf16[512,2304]{1,0:T(8,128)(2,1)}, bf16[512,2304]{1,0:T(8,128)(2,1)}) custom-call(bf16[1024,1024]{1,0:T(8,128)(2,1)} %copy-done.55, bf16[1024,1024]{1,0:T(8,128)(2,1)} %convolution_convert_fusion.5.ht, bf16[1024,1024]{1,0:T(8,128)(2,1)} %e.11, ...), custom_call_target="tpu_custom_call" | custom-call | flops 6442450944 | bytes 1048576 | tf_op jit(solution)/shard_map/pallas_call | solution.py:212
  237.8 13.0 %collective-permute-done.21 = bf16[64,2304]{1,0:T(8,128)(2,1)S(1)} collective-permute-done((bf16[64,2304]{1,0:T(8,128)(2,1)S(1)}, bf16[64,2304]{1,0:T(8,128)(2,1)S(1)}, u32[]{:S(2)}, u32[]{:S(2)}) %collective-permute-start.21) | collective-permute-done | bytes 294944 | tf_op jit(solution)/shard_map/ppermute | solution.py:283
  258.0 11.6 %collective-permute-done.19 = bf16[128,2304]{1,0:T(8,128)(2,1)S(1)} collective-permute-done((bf16[128,2304]{1,0:T(8,128)(2,1)S(1)}, bf16[128,2304]{1,0:T(8,128)(2,1)S(1)}, u32[]{:S(2)}, u32[]{:S(2)}) %collective-permute-start.19) | collective-permute-done | bytes 589856 | tf_op jit(solution)/shard_map/ppermute | solution.py:283
  272.5 23.3 %shard_map.181 = (bf16[1024,1024]{1,0:T(8,128)(2,1)}, bf16[1024,1024]{1,0:T(8,128)(2,1)}, bf16[512,2304]{1,0:T(8,128)(2,1)}, bf16[512,2304]{1,0:T(8,128)(2,1)}) custom-call(bf16[1024,1024]{1,0:T(8,128)(2,1)} %copy-done.55, bf16[1024,1024]{1,0:T(8,128)(2,1)} %convolution_convert_fusion.5.ht, bf16[1024,1024]{1,0:T(8,128)(2,1)} %e.11, ...), custom_call_target="tpu_custom_call" | custom-call | flops 6442450944 | bytes 1048576 | tf_op jit(solution)/shard_map/pallas_call | solution.py:212
  298.6 23.6 %shard_map.182 = (bf16[1024,1024]{1,0:T(8,128)(2,1)}, bf16[1024,1024]{1,0:T(8,128)(2,1)}, bf16[512,2304]{1,0:T(8,128)(2,1)}, bf16[512,2304]{1,0:T(8,128)(2,1)}) custom-call(bf16[1024,1024]{1,0:T(8,128)(2,1)} %copy-done.55, bf16[1024,1024]{1,0:T(8,128)(2,1)} %convolution_convert_fusion.5.ht, bf16[1024,1024]{1,0:T(8,128)(2,1)} %e.11, ...), custom_call_target="tpu_custom_call" | custom-call | flops 6442450944 | bytes 1048576 | tf_op jit(solution)/shard_map/pallas_call | solution.py:212
  323.6 8.6 %convert_add_fusion.1 = f32[1024,1024]{1,0:T(8,128)} fusion(bf16[1024,1024]{1,0:T(8,128)(2,1)} %get-tuple-element.152, bf16[1024,1024]{1,0:T(8,128)(2,1)} %get-tuple-element.151, bf16[1024,1024]{1,0:T(8,128)(2,1)} %get-tuple-element.150, bf16[1024,1024]{1,0:T(8,128)(2,1)} %get-tuple-element.149, bf16[1024,1024]{1,0:T(8,128)(2,1)S(1)} %copy-done.59, ...), kind=kLoop, calls=%fused_computation.59 | loop fusion | flops 11534336 | bytes 16777216 | tf_op jit(solution)/shard_map/add | solution.py:541
  362.4 7.4 %multiply_reduce_fusion.6 = (f32[512]{0:T(512)S(1)}, f32[512]{0:T(512)S(1)}, f32[512]{0:T(512)S(1)}, f32[1024,512]{1,0:T(8,128)S(1)}, bf16[1024,512]{1,0:T(8,128...) fusion(f32[1024,512]{1,0:T(8,128)S(1)} %slice_multiply_fusion.2, ...), kind=kOutput, calls=%fused_computation.96 | convolution fusion | flops 1087370240 | bytes 32507904 | tf_op jit(solution)/shard_map/dot_general | solution.py:27
  408.7 5.7 fusion.9
  416.1 9.6 %fusion.8 = (f32[1024,1024]{1,0:T(8,128)}, bf16[1024,1024]{1,0:T(8,128)(2,1)}) fusion(bf16[1024,1024]{1,0:T(8,128)(2,1)S(1)} %copy-done.18, f32[1024,1024]{1,0:T(8,128)} %get-tuple-element.297, f32[1024]{0:T(1024)S(1)} %broadcast_multiply_fusion, f32[1024]{0:T(1024)S(1)} %copy-done.75, f32[1024]{0:T(1024)S(1)} %copy-done.73, ...), kind=kLoop, calls=%fused_computation.23 | loop fusion | flops 28311552 | bytes 35676160 | tf_op jit(solution)/shard_map/add | solution.py:574
  429.1 19.3 %collective-permute-done.36 = bf16[128,2304]{1,0:T(8,128)(2,1)} collective-permute-done((bf16[128,2304]{1,0:T(8,128)(2,1)}, bf16[128,2304]{1,0:T(8,128)(2,1)}, u32[]{:S(2)}, u32[]{:S(2)}) %collective-permute-start.36) | collective-permute-done | bytes 589856 | tf_op jit(solution)/shard_map/ppermute | solution.py:283
  451.4 14.1 %collective-permute-done.40 = bf16[64,2304]{1,0:T(8,128)(2,1)S(1)} collective-permute-done((bf16[64,2304]{1,0:T(8,128)(2,1)S(1)}, bf16[64,2304]{1,0:T(8,128)(2,1)S(1)}, u32[]{:S(2)}, u32[]{:S(2)}) %collective-permute-start.40) | collective-permute-done | bytes 294944 | tf_op jit(solution)/shard_map/ppermute | solution.py:283
  469.9 8.2 %collective-permute-done.41 = bf16[256,2304]{1,0:T(8,128)(2,1)} collective-permute-done((bf16[256,2304]{1,0:T(8,128)(2,1)}, bf16[256,2304]{1,0:T(8,128)(2,1)}, u32[]{:S(2)}, u32[]{:S(2)}) %collective-permute-start.41) | collective-permute-done | bytes 1179680 | tf_op jit(solution)/shard_map/ppermute | solution.py:283
  484.6 19.6 %collective-permute-done.39 = bf16[512,1024]{1,0:T(8,128)(2,1)S(1)} collective-permute-done((bf16[512,1024]{1,0:T(8,128)(2,1)}, bf16[512,1024]{1,0:T(8,128)(2,1)S(1)}, u32[]{:S(2)}, u32[]{:S(2)}) %collective-permute-start.39) | collective-permute-done | bytes 1048608 | tf_op jit(solution)/shard_map/ppermute | solution.py:287
  509.4 18.5 %collective-permute-done.42 = bf16[128,1024]{1,0:T(8,128)(2,1)S(1)} collective-permute-done((bf16[128,1024]{1,0:T(8,128)(2,1)S(1)}, bf16[128,1024]{1,0:T(8,128)(2,1)S(1)}, u32[]{:S(2)}, u32[]{:S(2)}) %collective-permute-start.42) | collective-permute-done | bytes 262176 | tf_op jit(solution)/shard_map/ppermute | solution.py:283
  528.2 9.0 %collective-permute-done.48 = bf16[64,2304]{1,0:T(8,128)(2,1)S(1)} collective-permute-done((bf16[64,2304]{1,0:T(8,128)(2,1)S(1)}, bf16[64,2304]{1,0:T(8,128)(2,1)S(1)}, u32[]{:S(2)}, u32[]{:S(2)}) %collective-permute-start.48) | collective-permute-done | bytes 294944 | tf_op jit(solution)/shard_map/ppermute | solution.py:283
  538.0 7.8 %collective-permute-done.46 = bf16[128,1024]{1,0:T(8,128)(2,1)S(1)} collective-permute-done((bf16[128,1024]{1,0:T(8,128)(2,1)S(1)}, bf16[128,1024]{1,0:T(8,128)(2,1)S(1)}, u32[]{:S(2)}, u32[]{:S(2)}) %collective-permute-start.46) | collective-permute-done | bytes 262176 | tf_op jit(solution)/shard_map/ppermute | solution.py:283
  558.6 5.8 collective-permute-done.47
  573.0 11.3 %collective-permute-done.50 = bf16[128,1024]{1,0:T(8,128)(2,1)S(1)} collective-permute-done((bf16[128,1024]{1,0:T(8,128)(2,1)S(1)}, bf16[128,1024]{1,0:T(8,128)(2,1)S(1)}, u32[]{:S(2)}, u32[]{:S(2)}) %collective-permute-start.50) | collective-permute-done | bytes 262176 | tf_op jit(solution)/shard_map/ppermute | solution.py:283
  590.2 6.5 %collective-permute-done.30 = f32[10,512]{1,0:T(8,128)S(1)} collective-permute-done((f32[10,512]{1,0:T(8,128)S(1)}, f32[10,512]{1,0:T(8,128)S(1)}, u32[]{:S(2)}, u32[]{:S(2)}) %collective-permute-start.30) | collective-permute-done | bytes 20512 | tf_op jit(solution)/shard_map/ppermute | solution.py:283
  596.7 6.3 collective-permute-done.31
  603.0 13.8 %collective-permute-done.32 = f32[10,512]{1,0:T(8,128)S(1)} collective-permute-done((f32[10,512]{1,0:T(8,128)S(1)}, f32[10,512]{1,0:T(8,128)S(1)}, u32[]{:S(2)}, u32[]{:S(2)}) %collective-permute-start.32) | collective-permute-done | bytes 20512 | tf_op jit(solution)/shard_map/ppermute | solution.py:283
  622.3 6.7 %shard_map.185 = (f32[3,1024,512]{2,1,0:T(8,128)}, f32[512,1024]{1,0:T(8,128)}) custom-call(bf16[512,1024]{1,0:T(8,128)(2,1)S(1)} %pad_maximum_fusion.14.own1, bf16[512,1024]{1,0:T(8,128)(2,1)S(1)} %collective-permute-done.54.other1, bf16[512,1024]{1,0:T(8,128)(2,1)S(1)} %pad_maximum_fusion.15.own2, bf16[512,1024]{1,0:T(8,128)(2,1)S(1)} %collective-permute-done.56.other2, ...), custom_call_target="tpu_custom_call" | custom-call | flops 1048576 | bytes 1048576 | tf_op jit(solution)/shard_map/pallas_call | solution.py:358
  (402 shorter events, 226.9 us)
Async XLA Ops:
  7.2 57.8 %all-gather.6.cloned.1.call-start = ((), (), s32[]{:S(2)}) async-start(), calls=%async_computation | async-start | bytes 3342336 | tf_op jit(solution)/shard_map/all_gather | solution.py:435
  12.3 33.0 %collective-permute-start.2 = (bf16[256,1024]{1,0:T(8,128)(2,1)}, bf16[256,1024]{1,0:T(8,128)(2,1)}, u32[]{:S(2)}, u32[]{:S(2)}) collective-permute-start(bf16[256,1024]{1,0:T(8,128)(2,1)} %constant_dynamic-slice_fusion.1), channel_id=1, source_target_pairs={{0,1},{1,0},{2,3},{3,2},{4,5},{5,4},{6,7},{7,6},{8,9},{9,8},{10,11... | collective-permute-start | bytes 1572872 | tf_op jit(solution)/shard_map/ppermute | solution.py:287
  17.8 169.3 %all-gather.8.cloned.1.call-start = ((), (), s32[]{:S(2)}) async-start(), calls=%async_computation.1 | async-start | bytes 3342336 | tf_op jit(solution)/shard_map/all_gather | solution.py:435
  28.8 56.4 %collective-permute-start.4 = (bf16[512,1536]{1,0:T(8,128)(2,1)}, bf16[512,1536]{1,0:T(8,128)(2,1)}, u32[]{:S(2)}, u32[]{:S(2)}) collective-permute-start(bf16[512,1536]{1,0:T(8,128)(2,1)} %pad_maximum_fusion.9), channel_id=1, source_target_pairs={{0,1},{1,0},{2,3},{3,2},{4,5},{5,4},{6,7},{7,6},{8,9},{9,8},{10,11... | collective-permute-start | bytes 4718600 | tf_op jit(solution)/shard_map/ppermute | solution.py:287
  30.9 54.3 %collective-permute-start.5 = (bf16[384,1024]{1,0:T(8,128)(2,1)}, bf16[384,1024]{1,0:T(8,128)(2,1)}, u32[]{:S(2)}, u32[]{:S(2)}) collective-permute-start(bf16[384,1024]{1,0:T(8,128)(2,1)} %constant_dynamic-slice_fusion.2), channel_id=1, source_target_pairs={{0,1},{1,0},{2,3},{3,2},{4,5},{5,4},{6,7},{7,6},{8,9},{9,8},{10,11... | collective-permute-start | bytes 2359304 | tf_op jit(solution)/shard_map/ppermute | solution.py:287
  94.0 36.5 %collective-permute-start.9 = (bf16[512,1536]{1,0:T(8,128)(2,1)}, bf16[512,1536]{1,0:T(8,128)(2,1)}, u32[]{:S(2)}, u32[]{:S(2)}) collective-permute-start(bf16[512,1536]{1,0:T(8,128)(2,1)} %pad_maximum_fusion.10), channel_id=1, source_target_pairs={{0,1},{1,0},{2,3},{3,2},{4,5},{5,4},{6,7},{7,6},{8,9},{9,8},{10,11... | collective-permute-start | bytes 4718600 | tf_op jit(solution)/shard_map/ppermute | solution.py:287
  95.5 384.0 %all-gather.10.cloned.1.call-start = ((), (), s32[]{:S(2)}) async-start(), calls=%async_computation.2 | async-start | bytes 5013504 | tf_op jit(solution)/shard_map/all_gather | solution.py:332
  125.6 30.2 %collective-permute-start.10 = (bf16[512,2304]{1,0:T(8,128)(2,1)}, bf16[512,2304]{1,0:T(8,128)(2,1)}, u32[]{:S(2)}, u32[]{:S(2)}) collective-permute-start(bf16[512,2304]{1,0:T(8,128)(2,1)} %get-tuple-element.118), channel_id=1, source_target_pairs={{0,2},{2,0},{4,6},{6,4},{8,10},{10,8},{12,14},{14,12},{16,18},{18,... | collective-permute-start | bytes 7077896 | tf_op jit(solution)/shard_map/ppermute | solution.py:283
  130.5 28.0 %collective-permute-start.11 = (bf16[512,1536]{1,0:T(8,128)(2,1)}, bf16[512,1536]{1,0:T(8,128)(2,1)}, u32[]{:S(2)}, u32[]{:S(2)}) collective-permute-start(bf16[512,1536]{1,0:T(8,128)(2,1)} %collective-permute-done.9), channel_id=1, source_target_pairs={{0,2},{2,0},{4,6},{6,4},{8,10},{10,8},{12,14},{14,12},{16,18},{18,... | collective-permute-start | bytes 4718600 | tf_op jit(solution)/shard_map/ppermute | solution.py:283
  154.6 82.5 %collective-permute-start.17 = (bf16[512,1536]{1,0:T(8,128)(2,1)}, bf16[512,1536]{1,0:T(8,128)(2,1)}, u32[]{:S(2)}, u32[]{:S(2)}) collective-permute-start(bf16[512,1536]{1,0:T(8,128)(2,1)} %pad_maximum_fusion.12), channel_id=1, source_target_pairs={{0,1},{1,0},{2,3},{3,2},{4,5},{5,4},{6,7},{7,6},{8,9},{9,8},{10,11... | collective-permute-start | bytes 4718600 | tf_op jit(solution)/shard_map/ppermute | solution.py:287
  158.0 27.8 %collective-permute-start.13 = (bf16[256,2304]{1,0:T(8,128)(2,1)S(1)}, bf16[256,2304]{1,0:T(8,128)(2,1)S(1)}, u32[]{:S(2)}, u32[]{:S(2)}) collective-permute-start(bf16[256,2304]{1,0:T(8,128)(2,1)S(1)} %get-tuple-element.124), channel_id=1, source_target_pairs={{0,4},{2,6},{4,0},{6,2},{8,12},{10,14},{12,8},{14,10},{16,20},{18,... | collective-permute-start | bytes 3538952 | tf_op jit(solution)/shard_map/ppermute | solution.py:283
  210.3 25.8 %collective-permute-start.15 = (bf16[128,2304]{1,0:T(8,128)(2,1)S(1)}, bf16[128,2304]{1,0:T(8,128)(2,1)S(1)}, u32[]{:S(2)}, u32[]{:S(2)}) collective-permute-start(bf16[128,2304]{1,0:T(8,128)(2,1)S(1)} %copy-done.63), channel_id=1, source_target_pairs={{0,8},{2,10},{4,12},{6,14},{8,0},{10,2},{12,4},{14,6},{16,24},{18,... | collective-permute-start | bytes 1769480 | tf_op jit(solution)/shard_map/ppermute | solution.py:283
  212.2 40.4 %collective-permute-start.16 = (bf16[256,2304]{1,0:T(8,128)(2,1)}, bf16[256,2304]{1,0:T(8,128)(2,1)}, u32[]{:S(2)}, u32[]{:S(2)}) collective-permute-start(bf16[256,2304]{1,0:T(8,128)(2,1)} %get-tuple-element.129), channel_id=1, source_target_pairs={{0,4},{2,6},{4,0},{6,2},{8,12},{10,14},{12,8},{14,10},{16,20},{18,... | collective-permute-start | bytes 3538952 | tf_op jit(solution)/shard_map/ppermute | solution.py:283
  237.3 32.4 %collective-permute-start.14 = (bf16[512,2304]{1,0:T(8,128)(2,1)}, bf16[512,2304]{1,0:T(8,128)(2,1)S(1)}, u32[]{:S(2)}, u32[]{:S(2)}) collective-permute-start(bf16[512,2304]{1,0:T(8,128)(2,1)} %get-tuple-element.128), channel_id=1, source_target_pairs={{0,2},{2,0},{4,6},{6,4},{8,10},{10,8},{12,14},{14,12},{16,18},{18,... | collective-permute-start | bytes 7077896 | tf_op jit(solution)/shard_map/ppermute | solution.py:283
  237.8 58.9 %collective-permute-start.20 = (bf16[512,2304]{1,0:T(8,128)(2,1)}, bf16[512,2304]{1,0:T(8,128)(2,1)S(1)}, u32[]{:S(2)}, u32[]{:S(2)}) collective-permute-start(bf16[512,2304]{1,0:T(8,128)(2,1)} %get-tuple-element.134), channel_id=1, source_target_pairs={{0,2},{2,0},{4,6},{6,4},{8,10},{10,8},{12,14},{14,12},{16,18},{18,... | collective-permute-start | bytes 7077896 | tf_op jit(solution)/shard_map/ppermute | solution.py:283
  271.7 72.8 %collective-permute-start.23 = (bf16[512,2304]{1,0:T(8,128)(2,1)}, bf16[512,2304]{1,0:T(8,128)(2,1)}, u32[]{:S(2)}, u32[]{:S(2)}) collective-permute-start(bf16[512,2304]{1,0:T(8,128)(2,1)} %add_convert_fusion.3), channel_id=1, source_target_pairs={{0,1},{1,0},{2,3},{3,2},{4,5},{5,4},{6,7},{7,6},{8,9},{9,8},{10,11... | collective-permute-start | bytes 7077896 | tf_op jit(solution)/shard_map/ppermute | solution.py:287
  295.8 38.2 %collective-permute-start.22 = (bf16[512,2304]{1,0:T(8,128)(2,1)}, bf16[512,2304]{1,0:T(8,128)(2,1)}, u32[]{:S(2)}, u32[]{:S(2)}) collective-permute-start(bf16[512,2304]{1,0:T(8,128)(2,1)} %get-tuple-element.142), channel_id=1, source_target_pairs={{0,2},{2,0},{4,6},{6,4},{8,10},{10,8},{12,14},{14,12},{16,18},{18,... | collective-permute-start | bytes 7077896 | tf_op jit(solution)/shard_map/ppermute | solution.py:283
  295.8 36.3 %collective-permute-start.25 = (bf16[64,2304]{1,0:T(8,128)(2,1)S(1)}, bf16[64,2304]{1,0:T(8,128)(2,1)}, u32[]{:S(2)}, u32[]{:S(2)}) collective-permute-start(bf16[64,2304]{1,0:T(8,128)(2,1)S(1)} %add_convert_fusion.39), channel_id=1, source_target_pairs={{0,16},{2,18},{4,20},{6,22},{8,24},{10,26},{12,28},{14,30},{16,0},... | collective-permute-start | bytes 884744 | tf_op jit(solution)/shard_map/ppermute | solution.py:283
  338.5 87.2 %collective-permute-start.37 = (bf16[512,2304]{1,0:T(8,128)(2,1)}, bf16[512,2304]{1,0:T(8,128)(2,1)}, u32[]{:S(2)}, u32[]{:S(2)}) collective-permute-start(bf16[512,2304]{1,0:T(8,128)(2,1)} %add_convert_fusion.1), channel_id=1, source_target_pairs={{0,1},{1,0},{2,3},{3,2},{4,5},{5,4},{6,7},{7,6},{8,9},{9,8},{10,11... | collective-permute-start | bytes 7077896 | tf_op jit(solution)/shard_map/ppermute | solution.py:287
  348.9 47.1 %collective-permute-start.35 = (bf16[256,2304]{1,0:T(8,128)(2,1)}, bf16[256,2304]{1,0:T(8,128)(2,1)}, u32[]{:S(2)}, u32[]{:S(2)}) collective-permute-start(bf16[256,2304]{1,0:T(8,128)(2,1)} %get-tuple-element.158), channel_id=1, source_target_pairs={{0,4},{2,6},{4,0},{6,2},{8,12},{10,14},{12,8},{14,10},{16,20},{18,... | collective-permute-start | bytes 3538952 | tf_op jit(solution)/shard_map/ppermute | solution.py:283
  388.6 167.0 %all-gather.12.cloned.1.call-start = ((), (), s32[]{:S(2)}) async-start(), calls=%async_computation.3 | async-start | bytes 5013504 | tf_op jit(solution)/shard_map/all_gather | solution.py:332
  402.2 65.1 %collective-permute-start.34 = (bf16[512,1024]{1,0:T(8,128)(2,1)}, bf16[512,1024]{1,0:T(8,128)(2,1)}, u32[]{:S(2)}, u32[]{:S(2)}) collective-permute-start(bf16[512,1024]{1,0:T(8,128)(2,1)} %get-tuple-element.165), channel_id=1, source_target_pairs={{0,1},{1,0},{2,3},{3,2},{4,5},{5,4},{6,7},{7,6},{8,9},{9,8},{10,11... | collective-permute-start | bytes 3145736 | tf_op jit(solution)/shard_map/ppermute | solution.py:287
  414.4 34.0 %collective-permute-start.36 = (bf16[128,2304]{1,0:T(8,128)(2,1)}, bf16[128,2304]{1,0:T(8,128)(2,1)}, u32[]{:S(2)}, u32[]{:S(2)}) collective-permute-start(bf16[128,2304]{1,0:T(8,128)(2,1)} %get-tuple-element.169), channel_id=1, source_target_pairs={{0,8},{2,10},{4,12},{6,14},{8,0},{10,2},{12,4},{14,6},{16,24},{18,... | collective-permute-start | bytes 1769480 | tf_op jit(solution)/shard_map/ppermute | solution.py:283
  450.0 28.0 %collective-permute-start.41 = (bf16[256,2304]{1,0:T(8,128)(2,1)}, bf16[256,2304]{1,0:T(8,128)(2,1)}, u32[]{:S(2)}, u32[]{:S(2)}) collective-permute-start(bf16[256,2304]{1,0:T(8,128)(2,1)} %get-tuple-element.170), channel_id=1, source_target_pairs={{0,4},{2,6},{4,0},{6,2},{8,12},{10,14},{12,8},{14,10},{16,20},{18,... | collective-permute-start | bytes 3538952 | tf_op jit(solution)/shard_map/ppermute | solution.py:283
  479.6 149.4 %all-gather.14.cloned.1.call-start = ((), (), s32[]{:S(2)}) async-start(), calls=%async_computation.4 | async-start | bytes 5013504 | tf_op jit(solution)/shard_map/all_gather | solution.py:332
  479.9 24.3 %collective-permute-start.39 = (bf16[512,1024]{1,0:T(8,128)(2,1)}, bf16[512,1024]{1,0:T(8,128)(2,1)S(1)}, u32[]{:S(2)}, u32[]{:S(2)}) collective-permute-start(bf16[512,1024]{1,0:T(8,128)(2,1)} %get-tuple-element.166), channel_id=1, source_target_pairs={{0,1},{1,0},{2,3},{3,2},{4,5},{5,4},{6,7},{7,6},{8,9},{9,8},{10,11... | collective-permute-start | bytes 3145736 | tf_op jit(solution)/shard_map/ppermute | solution.py:287
  481.4 23.2 %collective-permute-start.38 = (bf16[256,1024]{1,0:T(8,128)(2,1)}, bf16[256,1024]{1,0:T(8,128)(2,1)S(1)}, u32[]{:S(2)}, u32[]{:S(2)}) collective-permute-start(bf16[256,1024]{1,0:T(8,128)(2,1)} %get-tuple-element.172), channel_id=1, source_target_pairs={{0,4},{2,6},{4,0},{6,2},{8,12},{10,14},{12,8},{14,10},{16,20},{18,... | collective-permute-start | bytes 1572872 | tf_op jit(solution)/shard_map/ppermute | solution.py:283
  482.4 26.1 %collective-permute-start.44 = (bf16[128,2304]{1,0:T(8,128)(2,1)S(1)}, bf16[128,2304]{1,0:T(8,128)(2,1)S(1)}, u32[]{:S(2)}, u32[]{:S(2)}) collective-permute-start(bf16[128,2304]{1,0:T(8,128)(2,1)S(1)} %get-tuple-element.173), channel_id=1, source_target_pairs={{0,8},{2,10},{4,12},{6,14},{8,0},{10,2},{12,4},{14,6},{16,24},{18,... | collective-permute-start | bytes 1769480 | tf_op jit(solution)/shard_map/ppermute | solution.py:283
  504.8 23.1 %collective-permute-start.43 = (bf16[256,1024]{1,0:T(8,128)(2,1)S(1)}, bf16[256,1024]{1,0:T(8,128)(2,1)S(1)}, u32[]{:S(2)}, u32[]{:S(2)}) collective-permute-start(bf16[256,1024]{1,0:T(8,128)(2,1)S(1)} %get-tuple-element.175), channel_id=1, source_target_pairs={{0,4},{2,6},{4,0},{6,2},{8,12},{10,14},{12,8},{14,10},{16,20},{18,... | collective-permute-start | bytes 1572872 | tf_op jit(solution)/shard_map/ppermute | solution.py:283
  508.6 28.6 %collective-permute-start.48 = (bf16[64,2304]{1,0:T(8,128)(2,1)S(1)}, bf16[64,2304]{1,0:T(8,128)(2,1)S(1)}, u32[]{:S(2)}, u32[]{:S(2)}) collective-permute-start(bf16[64,2304]{1,0:T(8,128)(2,1)S(1)} %add_convert_fusion.31), channel_id=1, source_target_pairs={{0,16},{2,18},{4,20},{6,22},{8,24},{10,26},{12,28},{14,30},{16,0},... | collective-permute-start | bytes 884744 | tf_op jit(solution)/shard_map/ppermute | solution.py:283
  584.3 33.3 %collective-permute-start.52 = (bf16[256,1024]{1,0:T(8,128)(2,1)S(1)}, bf16[256,1024]{1,0:T(8,128)(2,1)S(1)}, u32[]{:S(2)}, u32[]{:S(2)}) collective-permute-start(bf16[256,1024]{1,0:T(8,128)(2,1)S(1)} %pad_maximum_fusion.18), channel_id=1, source_target_pairs={{0,4},{2,6},{4,0},{6,2},{8,12},{10,14},{12,8},{14,10},{16,20},{18,... | collective-permute-start | bytes 1572872 | tf_op jit(solution)/shard_map/ppermute | solution.py:283
  587.2 30.6 %collective-permute-start.55 = (bf16[256,1024]{1,0:T(8,128)(2,1)S(1)}, bf16[256,1024]{1,0:T(8,128)(2,1)S(1)}, u32[]{:S(2)}, u32[]{:S(2)}) collective-permute-start(bf16[256,1024]{1,0:T(8,128)(2,1)S(1)} %pad_maximum_fusion.19), channel_id=1, source_target_pairs={{0,4},{2,6},{4,0},{6,2},{8,12},{10,14},{12,8},{14,10},{16,20},{18,... | collective-permute-start | bytes 1572872 | tf_op jit(solution)/shard_map/ppermute | solution.py:283
  (116 other events, 987.0 us)
Sparse Core Ops, SparseCore 0:
  17.9 47.0 all-gather.5
  95.7 43.4 all-gather.7
  388.7 59.6 all-gather.9
  479.7 66.8 all-gather.11
  555.7 68.3 all-gather.13

commit v3 on v2

--- a/solution.py
+++ b/solution.py
@@ -303,10 +303,11 @@
         self.dp, self.bit, self.terms = dp, bit, terms
 
     def halve(self, *others):
-        half = self.terms[0].shape[0] // 2
-        total = after(add(*[t[half:] for t in self.terms]), *others)
+        terms = after(self.terms, *others)
+        half = terms[0].shape[0] // 2
+        total = add(*[t[half:] for t in terms])
         self.bit += 1
-        self.terms = [add(*[t[:half] for t in self.terms]), swap(total, self.dp, self.bit)]
+        self.terms = [add(*[t[:half] for t in terms]), swap(total, self.dp, self.bit)]
         return total
 
     def total(self):

time: 646 us -> 617 us (0.955)
  waiting for transfers between devices: 208 us -> 174 us
    ppermute x43, waiting for transfers between devices: 170 us -> 136 us  [swap(): return lax.ppermute(values, 'dp', [(i, i ^ 1 << bit) for i in range(dp)])]
    unnamed x173 -> x155, local copies, waits for them, and re-layouts: 24.2 us -> 24.7 us
  transfers between devices with their start and end apart: 62 -> 62, of which waited for: 23 -> 22; matrix products, arithmetic and copies ran while one was open for 29% -> 28% of each run, Pallas kernels for 24% -> 25%
where the time goes in v3:
time: 617 us; the launch traced here: 614 us
  waiting for transfers between devices  174 us (28%)
  Pallas kernels  159 us (26%)
  other arithmetic  111 us (18%)
  matrix products  63.8 us (10%)
  starting transfers between devices  52.1 us (8%)
  local copies, waits for them, and re-layouts  38.2 us (6%)
  between operations  15.1 us (2%)
    pallas_call x6, Pallas kernels, ffn_part(): pl.pallas_call(ffn_body, grid=(count,), in_specs=[whole((rows, width)), w...  140 us
    ppermute x43, waiting for transfers between devices, swap(): return lax.ppermute(values, 'dp', [(i, i ^ 1 << bit) for i in range(dp)])  136 us
    convert_element_type x30, other arithmetic, add(): return total.astype(terms[0].dtype)  48.6 us
    dot_general x8, matrix products, right_outer(): lax.dot_general(left, right, (((1,), (1,)), ((), ())), preferred_element_...  38 us
    ppermute x43, starting transfers between devices, swap(): return lax.ppermute(values, 'dp', [(i, i ^ 1 << bit) for i in range(dp)])  32.9 us
    ppermute x14, waiting for transfers between devices, cross(): lax.ppermute(v, 'tensor', [(0, 1), (1, 0)])  26.5 us
    dot_general x12, matrix products, times_rows(): return jnp.dot(left, right, preferred_element_type=jnp.float32)  25.9 us
    unnamed x155, local copies, waits for them, and re-layouts  24.7 us
  transfers between devices with their start and end apart: 62, of which 22 were waited for; matrix products, arithmetic and copies ran while one was open for 28% of the time, Pallas kernels for 25%

profile of v3, /device:TPU:0, one launch (start us, length us, event | category | flops | bytes accessed | tf_op | source)
XLA Modules:
  0.0 613.5 jit_solution(4564521880149348718)
XLA Ops:
  31.1 4.8 copy.33
  35.9 4.7 convolution_convert_fusion.6
  40.5 4.8 convolution_convert_fusion.7.et
  53.6 11.4 %all-gather.6.cloned.1.call-done = bf16[1024,1536]{1,0:T(8,128)(2,1)} async-done(((bf16[64,1536]{1,0:T(8,128)(2,1)}), bf16[1024,1536]{1,0:T(8,128)(2,1)}) %all-gather.6.cloned.1.call-update) | async-done | bytes 3145744 | tf_op jit(solution)/shard_map/all_gather | solution.py:436
  65.0 5.9 fusion.79
  88.9 5.1 convolution_convert_fusion.5.ht
  102.4 23.3 %shard_map.177 = (bf16[1024,1024]{1,0:T(8,128)(2,1)}, bf16[1024,1024]{1,0:T(8,128)(2,1)}, bf16[512,2304]{1,0:T(8,128)(2,1)}, bf16[512,2304]{1,0:T(8,128)(2,1)}) custom-call(bf16[1024,1024]{1,0:T(8,128)(2,1)} %copy-done.49, bf16[1024,1024]{1,0:T(8,128)(2,1)} %convolution_convert_fusion.5.ht, bf16[1024,1024]{1,0:T(8,128)(2,1)} %e.11, ...), custom_call_target="tpu_custom_call" | custom-call | flops 6442450944 | bytes 1048576 | tf_op jit(solution)/shard_map/pallas_call | solution.py:212
  125.7 5.0 collective-permute-done.9
  132.9 23.5 %shard_map.178 = (bf16[1024,1024]{1,0:T(8,128)(2,1)}, bf16[1024,1024]{1,0:T(8,128)(2,1)}, bf16[512,2304]{1,0:T(8,128)(2,1)}, bf16[512,2304]{1,0:T(8,128)(2,1)}) custom-call(bf16[1024,1024]{1,0:T(8,128)(2,1)} %copy-done.49, bf16[1024,1024]{1,0:T(8,128)(2,1)} %convolution_convert_fusion.5.ht, bf16[1024,1024]{1,0:T(8,128)(2,1)} %e.11, ...), custom_call_target="tpu_custom_call" | custom-call | flops 6442450944 | bytes 1048576 | tf_op jit(solution)/shard_map/pallas_call | solution.py:212
  163.1 23.2 %shard_map.179 = (bf16[1024,1024]{1,0:T(8,128)(2,1)}, bf16[1024,1024]{1,0:T(8,128)(2,1)}, bf16[512,2304]{1,0:T(8,128)(2,1)}, bf16[512,2304]{1,0:T(8,128)(2,1)}) custom-call(bf16[1024,1024]{1,0:T(8,128)(2,1)} %copy-done.49, bf16[1024,1024]{1,0:T(8,128)(2,1)} %convolution_convert_fusion.5.ht, bf16[1024,1024]{1,0:T(8,128)(2,1)} %e.11, ...), custom_call_target="tpu_custom_call" | custom-call | flops 6442450944 | bytes 1048576 | tf_op jit(solution)/shard_map/pallas_call | solution.py:212
  194.7 23.1 %shard_map.180 = (bf16[1024,1024]{1,0:T(8,128)(2,1)}, bf16[1024,1024]{1,0:T(8,128)(2,1)}, bf16[512,2304]{1,0:T(8,128)(2,1)}, bf16[512,2304]{1,0:T(8,128)(2,1)}) custom-call(bf16[1024,1024]{1,0:T(8,128)(2,1)} %copy-done.49, bf16[1024,1024]{1,0:T(8,128)(2,1)} %convolution_convert_fusion.5.ht, bf16[1024,1024]{1,0:T(8,128)(2,1)} %e.11, ...), custom_call_target="tpu_custom_call" | custom-call | flops 6442450944 | bytes 1048576 | tf_op jit(solution)/shard_map/pallas_call | solution.py:212
  220.4 14.0 %collective-permute-done.21 = bf16[64,2304]{1,0:T(8,128)(2,1)S(1)} collective-permute-done((bf16[64,2304]{1,0:T(8,128)(2,1)S(1)}, bf16[64,2304]{1,0:T(8,128)(2,1)S(1)}, u32[]{:S(2)}, u32[]{:S(2)}) %collective-permute-start.21) | collective-permute-done | bytes 294944 | tf_op jit(solution)/shard_map/ppermute | solution.py:283
  245.1 23.7 %shard_map.181 = (bf16[1024,1024]{1,0:T(8,128)(2,1)}, bf16[1024,1024]{1,0:T(8,128)(2,1)}, bf16[512,2304]{1,0:T(8,128)(2,1)}, bf16[512,2304]{1,0:T(8,128)(2,1)}) custom-call(bf16[1024,1024]{1,0:T(8,128)(2,1)} %copy-done.49, bf16[1024,1024]{1,0:T(8,128)(2,1)} %convolution_convert_fusion.5.ht, bf16[1024,1024]{1,0:T(8,128)(2,1)} %e.11, ...), custom_call_target="tpu_custom_call" | custom-call | flops 6442450944 | bytes 1048576 | tf_op jit(solution)/shard_map/pallas_call | solution.py:212
  274.3 23.5 %shard_map.182 = (bf16[1024,1024]{1,0:T(8,128)(2,1)}, bf16[1024,1024]{1,0:T(8,128)(2,1)}, bf16[512,2304]{1,0:T(8,128)(2,1)}, bf16[512,2304]{1,0:T(8,128)(2,1)}) custom-call(bf16[1024,1024]{1,0:T(8,128)(2,1)} %copy-done.49, bf16[1024,1024]{1,0:T(8,128)(2,1)} %convolution_convert_fusion.5.ht, bf16[1024,1024]{1,0:T(8,128)(2,1)} %e.11, ...), custom_call_target="tpu_custom_call" | custom-call | flops 6442450944 | bytes 1048576 | tf_op jit(solution)/shard_map/pallas_call | solution.py:212
  298.9 8.5 %convert_add_fusion.1 = f32[1024,1024]{1,0:T(8,128)} fusion(bf16[1024,1024]{1,0:T(8,128)(2,1)} %get-tuple-element.176, bf16[1024,1024]{1,0:T(8,128)(2,1)} %get-tuple-element.175, bf16[1024,1024]{1,0:T(8,128)(2,1)} %get-tuple-element.174, bf16[1024,1024]{1,0:T(8,128)(2,1)} %get-tuple-element.173, bf16[1024,1024]{1,0:T(8,128)(2,1)S(1)} %copy-done.53, ...), kind=kLoop, calls=%fused_computation.59 | loop fusion | flops 11534336 | bytes 16777216 | tf_op jit(solution)/shard_map/add | solution.py:542
  309.3 4.5 add_convert_fusion.1
  320.8 4.3 add_convert_fusion.7
  337.3 7.5 %multiply_reduce_fusion.6 = (f32[512]{0:T(512)S(1)}, f32[512]{0:T(512)S(1)}, f32[512]{0:T(512)S(1)}, f32[1024,512]{1,0:T(8,128)S(1)}, bf16[1024,512]{1,0:T(8,128...) fusion(f32[1024,512]{1,0:T(8,128)S(1)} %slice_multiply_fusion.2, ...), kind=kOutput, calls=%fused_computation.96 | convolution fusion | flops 1087370240 | bytes 32507904 | tf_op jit(solution)/shard_map/dot_general | solution.py:27
  378.3 5.9 fusion.9
  386.7 10.0 %fusion.8 = (f32[1024,1024]{1,0:T(8,128)}, bf16[1024,1024]{1,0:T(8,128)(2,1)}) fusion(bf16[1024,1024]{1,0:T(8,128)(2,1)S(1)} %copy-done.18, f32[1024,1024]{1,0:T(8,128)} %get-tuple-element.333, f32[1024]{0:T(1024)S(1)} %broadcast_multiply_fusion, f32[1024]{0:T(1024)S(1)} %copy-done.66, f32[1024]{0:T(1024)S(1)} %copy-done.64, ...), kind=kLoop, calls=%fused_computation.23 | loop fusion | flops 28311552 | bytes 35676160 | tf_op jit(solution)/shard_map/add | solution.py:575
  400.0 15.4 %collective-permute-done.36 = bf16[128,2304]{1,0:T(8,128)(2,1)} collective-permute-done((bf16[128,2304]{1,0:T(8,128)(2,1)}, bf16[128,2304]{1,0:T(8,128)(2,1)}, u32[]{:S(2)}, u32[]{:S(2)}) %collective-permute-start.36) | collective-permute-done | bytes 589856 | tf_op jit(solution)/shard_map/ppermute | solution.py:283
  418.5 13.9 %collective-permute-done.40 = bf16[64,2304]{1,0:T(8,128)(2,1)S(1)} collective-permute-done((bf16[64,2304]{1,0:T(8,128)(2,1)S(1)}, bf16[64,2304]{1,0:T(8,128)(2,1)S(1)}, u32[]{:S(2)}, u32[]{:S(2)}) %collective-permute-start.40) | collective-permute-done | bytes 294944 | tf_op jit(solution)/shard_map/ppermute | solution.py:283
  436.7 8.1 %collective-permute-done.41 = bf16[256,2304]{1,0:T(8,128)(2,1)} collective-permute-done((bf16[256,2304]{1,0:T(8,128)(2,1)}, bf16[256,2304]{1,0:T(8,128)(2,1)}, u32[]{:S(2)}, u32[]{:S(2)}) %collective-permute-start.41) | collective-permute-done | bytes 1179680 | tf_op jit(solution)/shard_map/ppermute | solution.py:283
  451.9 18.6 %collective-permute-done.39 = bf16[512,1024]{1,0:T(8,128)(2,1)S(1)} collective-permute-done((bf16[512,1024]{1,0:T(8,128)(2,1)}, bf16[512,1024]{1,0:T(8,128)(2,1)S(1)}, u32[]{:S(2)}, u32[]{:S(2)}) %collective-permute-start.39) | collective-permute-done | bytes 1048608 | tf_op jit(solution)/shard_map/ppermute | solution.py:287
  476.6 12.7 %collective-permute-done.43 = bf16[256,1024]{1,0:T(8,128)(2,1)S(1)} collective-permute-done((bf16[256,1024]{1,0:T(8,128)(2,1)S(1)}, bf16[256,1024]{1,0:T(8,128)(2,1)S(1)}, u32[]{:S(2)}, u32[]{:S(2)}) %collective-permute-start.43) | collective-permute-done | bytes 524320 | tf_op jit(solution)/shard_map/ppermute | solution.py:283
  493.0 6.3 %collective-permute-done.48 = bf16[64,2304]{1,0:T(8,128)(2,1)S(1)} collective-permute-done((bf16[64,2304]{1,0:T(8,128)(2,1)S(1)}, bf16[64,2304]{1,0:T(8,128)(2,1)S(1)}, u32[]{:S(2)}, u32[]{:S(2)}) %collective-permute-start.48) | collective-permute-done | bytes 294944 | tf_op jit(solution)/shard_map/ppermute | solution.py:283
  503.4 11.3 %collective-permute-done.46 = bf16[128,1024]{1,0:T(8,128)(2,1)S(1)} collective-permute-done((bf16[128,1024]{1,0:T(8,128)(2,1)S(1)}, bf16[128,1024]{1,0:T(8,128)(2,1)S(1)}, u32[]{:S(2)}, u32[]{:S(2)}) %collective-permute-start.46) | collective-permute-done | bytes 262176 | tf_op jit(solution)/shard_map/ppermute | solution.py:283
  541.7 11.9 %collective-permute-done.50 = bf16[128,1024]{1,0:T(8,128)(2,1)S(1)} collective-permute-done((bf16[128,1024]{1,0:T(8,128)(2,1)S(1)}, bf16[128,1024]{1,0:T(8,128)(2,1)S(1)}, u32[]{:S(2)}, u32[]{:S(2)}) %collective-permute-start.50) | collective-permute-done | bytes 262176 | tf_op jit(solution)/shard_map/ppermute | solution.py:283
  558.0 6.1 collective-permute-done.30
  564.1 6.1 collective-permute-done.31
  572.4 14.4 %collective-permute-done.32 = f32[10,512]{1,0:T(8,128)S(1)} collective-permute-done((f32[10,512]{1,0:T(8,128)S(1)}, f32[10,512]{1,0:T(8,128)S(1)}, u32[]{:S(2)}, u32[]{:S(2)}) %collective-permute-start.32) | collective-permute-done | bytes 20512 | tf_op jit(solution)/shard_map/ppermute | solution.py:283
  593.7 6.7 %shard_map.185 = (f32[3,1024,512]{2,1,0:T(8,128)}, f32[512,1024]{1,0:T(8,128)}) custom-call(bf16[512,1024]{1,0:T(8,128)(2,1)S(1)} %pad_maximum_fusion.14.own1, bf16[512,1024]{1,0:T(8,128)(2,1)S(1)} %collective-permute-done.54.other1, bf16[512,1024]{1,0:T(8,128)(2,1)S(1)} %pad_maximum_fusion.15.own2, bf16[512,1024]{1,0:T(8,128)(2,1)S(1)} %collective-permute-done.56.other2, ...), custom_call_target="tpu_custom_call" | custom-call | flops 1048576 | bytes 1048576 | tf_op jit(solution)/shard_map/pallas_call | solution.py:359
  (384 shorter events, 230.4 us)
Async XLA Ops:
  7.2 57.8 %all-gather.6.cloned.1.call-start = ((), (), s32[]{:S(2)}) async-start(), calls=%async_computation | async-start | bytes 3342336 | tf_op jit(solution)/shard_map/all_gather | solution.py:436
  12.3 33.0 %collective-permute-start.2 = (bf16[256,1024]{1,0:T(8,128)(2,1)}, bf16[256,1024]{1,0:T(8,128)(2,1)}, u32[]{:S(2)}, u32[]{:S(2)}) collective-permute-start(bf16[256,1024]{1,0:T(8,128)(2,1)} %constant_dynamic-slice_fusion.1), channel_id=1, source_target_pairs={{0,1},{1,0},{2,3},{3,2},{4,5},{5,4},{6,7},{7,6},{8,9},{9,8},{10,11... | collective-permute-start | bytes 1572872 | tf_op jit(solution)/shard_map/ppermute | solution.py:287
  17.8 145.3 %all-gather.8.cloned.1.call-start = ((), (), s32[]{:S(2)}) async-start(), calls=%async_computation.1 | async-start | bytes 3342336 | tf_op jit(solution)/shard_map/all_gather | solution.py:436
  28.9 56.3 %collective-permute-start.4 = (bf16[512,1536]{1,0:T(8,128)(2,1)}, bf16[512,1536]{1,0:T(8,128)(2,1)}, u32[]{:S(2)}, u32[]{:S(2)}) collective-permute-start(bf16[512,1536]{1,0:T(8,128)(2,1)} %pad_maximum_fusion.9), channel_id=1, source_target_pairs={{0,1},{1,0},{2,3},{3,2},{4,5},{5,4},{6,7},{7,6},{8,9},{9,8},{10,11... | collective-permute-start | bytes 4718600 | tf_op jit(solution)/shard_map/ppermute | solution.py:287
  31.0 54.2 %collective-permute-start.5 = (bf16[384,1024]{1,0:T(8,128)(2,1)}, bf16[384,1024]{1,0:T(8,128)(2,1)}, u32[]{:S(2)}, u32[]{:S(2)}) collective-permute-start(bf16[384,1024]{1,0:T(8,128)(2,1)} %constant_dynamic-slice_fusion.2), channel_id=1, source_target_pairs={{0,1},{1,0},{2,3},{3,2},{4,5},{5,4},{6,7},{7,6},{8,9},{9,8},{10,11... | collective-permute-start | bytes 2359304 | tf_op jit(solution)/shard_map/ppermute | solution.py:287
  94.1 36.7 %collective-permute-start.9 = (bf16[512,1536]{1,0:T(8,128)(2,1)}, bf16[512,1536]{1,0:T(8,128)(2,1)}, u32[]{:S(2)}, u32[]{:S(2)}) collective-permute-start(bf16[512,1536]{1,0:T(8,128)(2,1)} %pad_maximum_fusion.10), channel_id=1, source_target_pairs={{0,1},{1,0},{2,3},{3,2},{4,5},{5,4},{6,7},{7,6},{8,9},{9,8},{10,11... | collective-permute-start | bytes 4718600 | tf_op jit(solution)/shard_map/ppermute | solution.py:287
  95.6 350.8 %all-gather.10.cloned.1.call-start = ((), (), s32[]{:S(2)}) async-start(), calls=%async_computation.2 | async-start | bytes 5013504 | tf_op jit(solution)/shard_map/all_gather | solution.py:333
  125.7 31.0 %collective-permute-start.10 = (bf16[512,2304]{1,0:T(8,128)(2,1)}, bf16[512,2304]{1,0:T(8,128)(2,1)S(1)}, u32[]{:S(2)}, u32[]{:S(2)}) collective-permute-start(bf16[512,2304]{1,0:T(8,128)(2,1)} %get-tuple-element.136), channel_id=1, source_target_pairs={{0,2},{2,0},{4,6},{6,4},{8,10},{10,8},{12,14},{14,12},{16,18},{18,... | collective-permute-start | bytes 7077896 | tf_op jit(solution)/shard_map/ppermute | solution.py:283
  130.7 28.4 %collective-permute-start.11 = (bf16[512,1536]{1,0:T(8,128)(2,1)}, bf16[512,1536]{1,0:T(8,128)(2,1)}, u32[]{:S(2)}, u32[]{:S(2)}) collective-permute-start(bf16[512,1536]{1,0:T(8,128)(2,1)} %collective-permute-done.9), channel_id=1, source_target_pairs={{0,2},{2,0},{4,6},{6,4},{8,10},{10,8},{12,14},{14,12},{16,18},{18,... | collective-permute-start | bytes 4718600 | tf_op jit(solution)/shard_map/ppermute | solution.py:283
  132.0 87.7 %collective-permute-start.17 = (bf16[512,1536]{1,0:T(8,128)(2,1)}, bf16[512,1536]{1,0:T(8,128)(2,1)}, u32[]{:S(2)}, u32[]{:S(2)}) collective-permute-start(bf16[512,1536]{1,0:T(8,128)(2,1)} %pad_maximum_fusion.12), channel_id=1, source_target_pairs={{0,1},{1,0},{2,3},{3,2},{4,5},{5,4},{6,7},{7,6},{8,9},{9,8},{10,11... | collective-permute-start | bytes 4718600 | tf_op jit(solution)/shard_map/ppermute | solution.py:287
  156.4 30.7 %collective-permute-start.12 = (bf16[512,2304]{1,0:T(8,128)(2,1)}, bf16[512,2304]{1,0:T(8,128)(2,1)}, u32[]{:S(2)}, u32[]{:S(2)}) collective-permute-start(bf16[512,2304]{1,0:T(8,128)(2,1)} %get-tuple-element.141), channel_id=1, source_target_pairs={{0,2},{2,0},{4,6},{6,4},{8,10},{10,8},{12,14},{14,12},{16,18},{18,... | collective-permute-start | bytes 7077896 | tf_op jit(solution)/shard_map/ppermute | solution.py:283
  158.6 28.4 %collective-permute-start.13 = (bf16[256,2304]{1,0:T(8,128)(2,1)}, bf16[256,2304]{1,0:T(8,128)(2,1)}, u32[]{:S(2)}, u32[]{:S(2)}) collective-permute-start(bf16[256,2304]{1,0:T(8,128)(2,1)} %get-tuple-element.265), channel_id=1, source_target_pairs={{0,4},{2,6},{4,0},{6,2},{8,12},{10,14},{12,8},{14,10},{16,20},{18,... | collective-permute-start | bytes 3538952 | tf_op jit(solution)/shard_map/ppermute | solution.py:283
  188.6 29.2 %collective-permute-start.15 = (bf16[128,2304]{1,0:T(8,128)(2,1)S(1)}, bf16[128,2304]{1,0:T(8,128)(2,1)}, u32[]{:S(2)}, u32[]{:S(2)}) collective-permute-start(bf16[128,2304]{1,0:T(8,128)(2,1)S(1)} %get-tuple-element.291), channel_id=1, source_target_pairs={{0,8},{2,10},{4,12},{6,14},{8,0},{10,2},{12,4},{14,6},{16,24},{18,... | collective-permute-start | bytes 1769480 | tf_op jit(solution)/shard_map/ppermute | solution.py:283
  193.7 42.6 %collective-permute-start.16 = (bf16[256,2304]{1,0:T(8,128)(2,1)}, bf16[256,2304]{1,0:T(8,128)(2,1)S(1)}, u32[]{:S(2)}, u32[]{:S(2)}) collective-permute-start(bf16[256,2304]{1,0:T(8,128)(2,1)} %get-tuple-element.263), channel_id=1, source_target_pairs={{0,4},{2,6},{4,0},{6,2},{8,12},{10,14},{12,8},{14,10},{16,20},{18,... | collective-permute-start | bytes 3538952 | tf_op jit(solution)/shard_map/ppermute | solution.py:283
  220.4 51.9 %collective-permute-start.20 = (bf16[512,2304]{1,0:T(8,128)(2,1)}, bf16[512,2304]{1,0:T(8,128)(2,1)S(1)}, u32[]{:S(2)}, u32[]{:S(2)}) collective-permute-start(bf16[512,2304]{1,0:T(8,128)(2,1)} %get-tuple-element.155), channel_id=1, source_target_pairs={{0,2},{2,0},{4,6},{6,4},{8,10},{10,8},{12,14},{14,12},{16,18},{18,... | collective-permute-start | bytes 7077896 | tf_op jit(solution)/shard_map/ppermute | solution.py:283
  237.6 31.2 %collective-permute-start.19 = (bf16[128,2304]{1,0:T(8,128)(2,1)}, bf16[128,2304]{1,0:T(8,128)(2,1)}, u32[]{:S(2)}, u32[]{:S(2)}) collective-permute-start(bf16[128,2304]{1,0:T(8,128)(2,1)} %get-tuple-element.289), channel_id=1, source_target_pairs={{0,8},{2,10},{4,12},{6,14},{8,0},{10,2},{12,4},{14,6},{16,24},{18,... | collective-permute-start | bytes 1769480 | tf_op jit(solution)/shard_map/ppermute | solution.py:283
  243.9 74.8 %collective-permute-start.23 = (bf16[512,2304]{1,0:T(8,128)(2,1)}, bf16[512,2304]{1,0:T(8,128)(2,1)}, u32[]{:S(2)}, u32[]{:S(2)}) collective-permute-start(bf16[512,2304]{1,0:T(8,128)(2,1)} %add_convert_fusion.3), channel_id=1, source_target_pairs={{0,1},{1,0},{2,3},{3,2},{4,5},{5,4},{6,7},{7,6},{8,9},{9,8},{10,11... | collective-permute-start | bytes 7077896 | tf_op jit(solution)/shard_map/ppermute | solution.py:287
  268.7 40.6 %collective-permute-start.22 = (bf16[512,2304]{1,0:T(8,128)(2,1)}, bf16[512,2304]{1,0:T(8,128)(2,1)}, u32[]{:S(2)}, u32[]{:S(2)}) collective-permute-start(bf16[512,2304]{1,0:T(8,128)(2,1)} %get-tuple-element.165), channel_id=1, source_target_pairs={{0,2},{2,0},{4,6},{6,4},{8,10},{10,8},{12,14},{14,12},{16,18},{18,... | collective-permute-start | bytes 7077896 | tf_op jit(solution)/shard_map/ppermute | solution.py:283
  269.9 37.5 %collective-permute-start.25 = (bf16[64,2304]{1,0:T(8,128)(2,1)S(1)}, bf16[64,2304]{1,0:T(8,128)(2,1)}, u32[]{:S(2)}, u32[]{:S(2)}) collective-permute-start(bf16[64,2304]{1,0:T(8,128)(2,1)S(1)} %add_convert_fusion.39), channel_id=1, source_target_pairs={{0,16},{2,18},{4,20},{6,22},{8,24},{10,26},{12,28},{14,30},{16,0},... | collective-permute-start | bytes 884744 | tf_op jit(solution)/shard_map/ppermute | solution.py:283
  335.4 48.7 %collective-permute-start.35 = (bf16[256,2304]{1,0:T(8,128)(2,1)}, bf16[256,2304]{1,0:T(8,128)(2,1)}, u32[]{:S(2)}, u32[]{:S(2)}) collective-permute-start(bf16[256,2304]{1,0:T(8,128)(2,1)} %get-tuple-element.261), channel_id=1, source_target_pairs={{0,4},{2,6},{4,0},{6,2},{8,12},{10,14},{12,8},{14,10},{16,20},{18,... | collective-permute-start | bytes 3538952 | tf_op jit(solution)/shard_map/ppermute | solution.py:283
  336.0 60.6 %collective-permute-start.37 = (bf16[512,2304]{1,0:T(8,128)(2,1)}, bf16[512,2304]{1,0:T(8,128)(2,1)}, u32[]{:S(2)}, u32[]{:S(2)}) collective-permute-start(bf16[512,2304]{1,0:T(8,128)(2,1)} %add_convert_fusion.1), channel_id=1, source_target_pairs={{0,1},{1,0},{2,3},{3,2},{4,5},{5,4},{6,7},{7,6},{8,9},{9,8},{10,11... | collective-permute-start | bytes 7077896 | tf_op jit(solution)/shard_map/ppermute | solution.py:287
  355.1 171.0 %all-gather.12.cloned.1.call-start = ((), (), s32[]{:S(2)}) async-start(), calls=%async_computation.3 | async-start | bytes 5013504 | tf_op jit(solution)/shard_map/all_gather | solution.py:333
  372.9 61.3 %collective-permute-start.34 = (bf16[512,1024]{1,0:T(8,128)(2,1)}, bf16[512,1024]{1,0:T(8,128)(2,1)}, u32[]{:S(2)}, u32[]{:S(2)}) collective-permute-start(bf16[512,1024]{1,0:T(8,128)(2,1)} %get-tuple-element.190), channel_id=1, source_target_pairs={{0,1},{1,0},{2,3},{3,2},{4,5},{5,4},{6,7},{7,6},{8,9},{9,8},{10,11... | collective-permute-start | bytes 3145736 | tf_op jit(solution)/shard_map/ppermute | solution.py:287
  386.6 28.8 %collective-permute-start.36 = (bf16[128,2304]{1,0:T(8,128)(2,1)}, bf16[128,2304]{1,0:T(8,128)(2,1)}, u32[]{:S(2)}, u32[]{:S(2)}) collective-permute-start(bf16[128,2304]{1,0:T(8,128)(2,1)} %get-tuple-element.286), channel_id=1, source_target_pairs={{0,8},{2,10},{4,12},{6,14},{8,0},{10,2},{12,4},{14,6},{16,24},{18,... | collective-permute-start | bytes 1769480 | tf_op jit(solution)/shard_map/ppermute | solution.py:283
  417.0 27.8 %collective-permute-start.41 = (bf16[256,2304]{1,0:T(8,128)(2,1)}, bf16[256,2304]{1,0:T(8,128)(2,1)}, u32[]{:S(2)}, u32[]{:S(2)}) collective-permute-start(bf16[256,2304]{1,0:T(8,128)(2,1)} %get-tuple-element.259), channel_id=1, source_target_pairs={{0,4},{2,6},{4,0},{6,2},{8,12},{10,14},{12,8},{14,10},{16,20},{18,... | collective-permute-start | bytes 3538952 | tf_op jit(solution)/shard_map/ppermute | solution.py:283
  446.4 154.0 %all-gather.14.cloned.1.call-start = ((), (), s32[]{:S(2)}) async-start(), calls=%async_computation.4 | async-start | bytes 5013504 | tf_op jit(solution)/shard_map/all_gather | solution.py:333
  448.0 24.4 %collective-permute-start.38 = (bf16[256,1024]{1,0:T(8,128)(2,1)}, bf16[256,1024]{1,0:T(8,128)(2,1)S(1)}, u32[]{:S(2)}, u32[]{:S(2)}) collective-permute-start(bf16[256,1024]{1,0:T(8,128)(2,1)} %get-tuple-element.294), channel_id=1, source_target_pairs={{0,4},{2,6},{4,0},{6,2},{8,12},{10,14},{12,8},{14,10},{16,20},{18,... | collective-permute-start | bytes 1572872 | tf_op jit(solution)/shard_map/ppermute | solution.py:283
  473.4 25.9 %collective-permute-start.48 = (bf16[64,2304]{1,0:T(8,128)(2,1)S(1)}, bf16[64,2304]{1,0:T(8,128)(2,1)S(1)}, u32[]{:S(2)}, u32[]{:S(2)}) collective-permute-start(bf16[64,2304]{1,0:T(8,128)(2,1)S(1)} %add_convert_fusion.31), channel_id=1, source_target_pairs={{0,16},{2,18},{4,20},{6,22},{8,24},{10,26},{12,28},{14,30},{16,0},... | collective-permute-start | bytes 884744 | tf_op jit(solution)/shard_map/ppermute | solution.py:283
  475.9 27.4 %collective-permute-start.42 = (bf16[128,1024]{1,0:T(8,128)(2,1)}, bf16[128,1024]{1,0:T(8,128)(2,1)S(1)}, u32[]{:S(2)}, u32[]{:S(2)}) collective-permute-start(bf16[128,1024]{1,0:T(8,128)(2,1)} %get-tuple-element.302), channel_id=1, source_target_pairs={{0,8},{2,10},{4,12},{6,14},{8,0},{10,2},{12,4},{14,6},{16,24},{18,... | collective-permute-start | bytes 786440 | tf_op jit(solution)/shard_map/ppermute | solution.py:283
  489.5 25.3 %collective-permute-start.46 = (bf16[128,1024]{1,0:T(8,128)(2,1)S(1)}, bf16[128,1024]{1,0:T(8,128)(2,1)S(1)}, u32[]{:S(2)}, u32[]{:S(2)}) collective-permute-start(bf16[128,1024]{1,0:T(8,128)(2,1)S(1)} %get-tuple-element.301), channel_id=1, source_target_pairs={{0,8},{2,10},{4,12},{6,14},{8,0},{10,2},{12,4},{14,6},{16,24},{18,... | collective-permute-start | bytes 786440 | tf_op jit(solution)/shard_map/ppermute | solution.py:283
  553.6 35.2 %collective-permute-start.52 = (bf16[256,1024]{1,0:T(8,128)(2,1)S(1)}, bf16[256,1024]{1,0:T(8,128)(2,1)S(1)}, u32[]{:S(2)}, u32[]{:S(2)}) collective-permute-start(bf16[256,1024]{1,0:T(8,128)(2,1)S(1)} %pad_maximum_fusion.18), channel_id=1, source_target_pairs={{0,4},{2,6},{4,0},{6,2},{8,12},{10,14},{12,8},{14,10},{16,20},{18,... | collective-permute-start | bytes 1572872 | tf_op jit(solution)/shard_map/ppermute | solution.py:283
  556.5 32.4 %collective-permute-start.55 = (bf16[256,1024]{1,0:T(8,128)(2,1)S(1)}, bf16[256,1024]{1,0:T(8,128)(2,1)S(1)}, u32[]{:S(2)}, u32[]{:S(2)}) collective-permute-start(bf16[256,1024]{1,0:T(8,128)(2,1)S(1)} %pad_maximum_fusion.19), channel_id=1, source_target_pairs={{0,4},{2,6},{4,0},{6,2},{8,12},{10,14},{12,8},{14,10},{16,20},{18,... | collective-permute-start | bytes 1572872 | tf_op jit(solution)/shard_map/ppermute | solution.py:283
  (107 other events, 919.4 us)
Sparse Core Ops, SparseCore 0:
  17.9 47.0 all-gather.5
  95.7 43.3 all-gather.7
  355.2 58.0 all-gather.9
  446.5 69.1 all-gather.11
  526.3 67.5 all-gather.13
